TPU v7x, 256 devices: a whole 4x4x8 slice. The times are simulated.
256 devices in a mesh: pipe: 16 (over x_hi, y, core), ctx: 16 (over x_lo, z).
Axes of the slice: x: 4 (x_hi: 2, x_lo: 2; x = x_hi * 2 + x_lo), y: 4, z: 8, core: 2. Of those that a mesh axis runs over, the one named last changes fastest.
Arguments:
- query: bfloat16 [16, 2048, 4096], P('pipe', 'ctx'), may hold values from -8 to 8
- key: bfloat16 [16, 2048, 512], P('pipe', 'ctx'), may hold values from -8 to 8
- value: bfloat16 [16, 2048, 512], P('pipe', 'ctx'), may hold values from -6 to 6
- out_grad: bfloat16 [16, 2048, 4096], P('pipe', 'ctx'), may hold values from -6 to 6
- positions: int32 [16, 2048], P('pipe', 'ctx'), may hold values from 0 to 2047, as said below
- gains: float32 [16, 2, 128], P('pipe'), may hold values from 0.5 to 5, as said below
Outputs:
- attended: bfloat16 [16, 2048, 4096], P('pipe', 'ctx')
- query_grad: bfloat16 [16, 2048, 4096], P('pipe', 'ctx')
- key_grad: bfloat16 [16, 2048, 512], P('pipe', 'ctx')
- value_grad: bfloat16 [16, 2048, 512], P('pipe', 'ctx')
- gain_grad: float32 [16, 2, 128], P('pipe')
Inputs may be any that keep to these rules, and one draw needn't show every extreme that they name: Row p holds the positions of sequence p, each position once; the 128 rows of one device are two runs of 64 consecutive, increasing positions that start at multiples of 64; the 32 runs may lie on the devices in any order. `gains`: rows p and 15 - p are equal.
All inputs are finite; a program needn't handle non-finite values.
Results may differ from a plain program's by a relative error of at most 0.03.
The roundings to bfloat16 on the way count: a program that leaves them out, or rounds other values in their place, can miss the bound.
Values may be sent and summed in bfloat16 or wider, within the bound.
No kernel may reach another device: no remote copies, remote signals or barrier semaphores. Data moves between devices by JAX's collectives and lax.ppermute only.
A program may use at most 192 MiB of HBM per device.

v0:
```python
import jax
import jax.numpy as jnp
from jax import lax
from jax.sharding import PartitionSpec as P

HQ = 32
HK = 4
DH = 128


THETA = 1000000.0
EPS = 1e-06
NEG = -1e30


def from_behind(array, axis, by):
    devices = lax.axis_size(axis)
    return lax.ppermute(array, axis, [(i, (i + by) % devices) for i in range(devices)])


def partner(value, axis, distance):
    mask = 2**distance
    pairs = [(source, source ^ mask) for source in range(lax.axis_size(axis))]
    return lax.ppermute(value, axis, pairs)


def angles(pos):
    freq = THETA ** (-(jnp.arange(DH // 2, dtype=jnp.float32) * 2.0) / DH)
    turn = pos.astype(jnp.float32)[:, None] * freq[None, :]
    return (jnp.cos(turn)[:, None, :], jnp.sin(turn)[:, None, :])


def rotate(x, cosine, sine):
    first, second = (x[..., : DH // 2], x[..., DH // 2 :])
    return jnp.concatenate([first * cosine - second * sine, second * cosine + first * sine], -1)


def unrotate(x, cosine, sine):
    first, second = (x[..., : DH // 2], x[..., DH // 2 :])
    return jnp.concatenate([first * cosine + second * sine, second * cosine - first * sine], -1)


def normalize(x, gain):
    inverse = lax.rsqrt(jnp.mean(x * x, -1, keepdims=True) + EPS)
    normed = x * inverse
    return (normed, inverse, normed * gain)


def norm_back(grad_scaled, normed, inverse, gain):
    grad_normed = grad_scaled * gain
    inner = jnp.mean(grad_normed * normed, -1, keepdims=True)
    return inverse * (grad_normed - normed * inner)


def body(query, key, value, out_grad, positions, gains):
    rows = query.shape[1]
    ratio = HQ // HK
    scale = DH ** (-0.5)
    count = lax.axis_size("ctx")
    here = lax.axis_index("ctx")
    every_pos = lax.all_gather(positions, "ctx", axis=1, tiled=True)[0]
    my_pos = positions[0]
    cosine, sine = angles(my_pos)
    gain = gains[0]
    q_normed, q_inverse, q_scaled = normalize(
        query[0].astype(jnp.float32).reshape(rows, HQ, DH), gain[0]
    )
    k_normed, k_inverse, k_scaled = normalize(
        key[0].astype(jnp.float32).reshape(rows, HK, DH), gain[1]
    )
    q_rot = rotate(q_scaled, cosine, sine).astype(jnp.bfloat16).reshape(rows, HK, ratio, DH)
    k_rot = rotate(k_scaled, cosine, sine).astype(jnp.bfloat16).reshape(rows, HK * DH)
    values = value[0]
    grads = out_grad[0].reshape(rows, HK, ratio, DH)

    def visible(key_pos):
        return key_pos[None, :] <= my_pos[:, None]

    start_state = (
        jnp.full((rows, HK, ratio), NEG, jnp.float32),
        jnp.zeros((rows, HK, ratio), jnp.float32),
        jnp.zeros((rows, HK, ratio, DH), jnp.float32),
    )
    k_piece = lax.all_gather(k_rot, "ctx", axis=0, tiled=True)
    v_piece = lax.all_gather(values, "ctx", axis=0, tiled=True)
    width = k_piece.shape[0]
    key_pos = every_pos
    mask = visible(key_pos)[:, None, None, :]

    def compute(state):
        top, total, accum = state
        k_head = k_piece.reshape(width, HK, DH)
        v_head = v_piece.reshape(width, HK, DH)
        scores = (
            jnp.einsum("qgrd,kgd->qgrk", q_rot, k_head, preferred_element_type=jnp.float32) * scale
        )
        scores = jnp.where(mask, scores, NEG)
        new_top = jnp.maximum(top, jnp.max(scores, -1))
        expo = jnp.where(mask, jnp.exp(scores - new_top[..., None]), 0.0)
        total = jnp.sum(expo, -1)
        accum = jnp.einsum(
            "qgrk,kgd->qgrd", expo.astype(jnp.bfloat16), v_head, preferred_element_type=jnp.float32
        )
        return (new_top, total, accum)

    def forward_keep(state):
        return state

    top, total, accum = lax.cond(jnp.any(mask), compute, forward_keep, start_state)
    attended = (accum / total[..., None]).astype(jnp.bfloat16)
    logsum = top + jnp.log(total)
    delta = jnp.sum(grads.astype(jnp.float32) * attended.astype(jnp.float32), -1)

    def grad_tile(k_block, v_block, key_pos):
        width = k_block.shape[0]
        k_head = k_block.reshape(width, HK, DH)
        v_head = v_block.reshape(width, HK, DH)
        mask = visible(key_pos)[:, None, None, :]
        scores = (
            jnp.einsum("qgrd,kgd->qgrk", q_rot, k_head, preferred_element_type=jnp.float32) * scale
        )
        probs = jnp.where(mask, jnp.exp(scores - logsum[..., None]), 0.0)
        d_value = jnp.einsum(
            "qgrk,qgrd->kgd", probs.astype(jnp.bfloat16), grads, preferred_element_type=jnp.float32
        )
        d_prob = jnp.einsum("qgrd,kgd->qgrk", grads, v_head, preferred_element_type=jnp.float32)
        d_score = (probs * (d_prob - delta[..., None])).astype(jnp.bfloat16)
        d_query = (
            jnp.einsum("qgrk,kgd->qgrd", d_score, k_head, preferred_element_type=jnp.float32)
            * scale
        )
        d_key = (
            jnp.einsum("qgrk,qgrd->kgd", d_score, q_rot, preferred_element_type=jnp.float32) * scale
        )
        return (d_query, d_key.reshape(width, HK * DH), d_value.reshape(width, HK * DH))

    dq_start = jnp.zeros((rows, HK, ratio, DH), jnp.float32)

    def cycle_step(step, state):
        k_buf, v_buf, dk_buf, dv_buf, dq_acc = state
        source = (here - step) % count
        key_pos = lax.dynamic_slice_in_dim(every_pos, source * rows, rows)

        def add_tile(inner):
            d_query, d_key, d_value = grad_tile(k_buf, v_buf, key_pos)
            return (inner[0] + d_query, inner[1] + d_key, inner[2] + d_value)

        def cycle_keep(inner):
            return inner

        dq_acc, dk_buf, dv_buf = lax.cond(
            jnp.any(visible(key_pos)), add_tile, cycle_keep, (dq_acc, dk_buf, dv_buf)
        )
        k_buf, v_buf = from_behind((k_buf, v_buf), "ctx", 1)
        dk_buf, dv_buf = (
            from_behind(dk_buf.astype(jnp.bfloat16), "ctx", 1).astype(dk_buf.dtype),
            from_behind(dv_buf.astype(jnp.bfloat16), "ctx", 1).astype(dv_buf.dtype),
        )
        return (k_buf, v_buf, dk_buf, dv_buf, dq_acc)

    grad_zero = jnp.zeros((rows, HK * DH), jnp.float32)
    cycle_out = lax.fori_loop(0, count, cycle_step, (k_rot, values, grad_zero, grad_zero, dq_start))
    dk_acc, dv_acc, dq_acc = (cycle_out[2], cycle_out[3], cycle_out[4])
    dq_scaled = unrotate(dq_acc.reshape(rows, HQ, DH), cosine, sine)
    dk_scaled = unrotate(dk_acc.reshape(rows, HK, DH), cosine, sine)
    query_grad = (
        norm_back(dq_scaled, q_normed, q_inverse, gain[0])
        .astype(jnp.bfloat16)
        .reshape(1, rows, HQ * DH)
    )
    key_grad = (
        norm_back(dk_scaled, k_normed, k_inverse, gain[1])
        .astype(jnp.bfloat16)
        .reshape(1, rows, HK * DH)
    )
    value_grad = dv_acc.astype(jnp.bfloat16).reshape(1, rows, HK * DH)
    own = jnp.stack(
        [jnp.sum(dq_scaled * q_normed, axis=(0, 1)), jnp.sum(dk_scaled * k_normed, axis=(0, 1))]
    )
    summed = lax.psum(own, "ctx")
    mirrored = summed
    for bit in range(lax.axis_size("pipe").bit_length() - 1):
        mirrored = partner(mirrored, "pipe", bit)
    gain_grad = summed + mirrored
    return (attended.reshape(1, rows, HQ * DH), query_grad, key_grad, value_grad, gain_grad[None])


def solution(mesh):
    in_specs = (
        P("pipe", "ctx", None),
        P("pipe", "ctx", None),
        P("pipe", "ctx", None),
        P("pipe", "ctx", None),
        P("pipe", "ctx"),
        P("pipe", None, None),
    )
    out_specs = (
        P("pipe", "ctx", None),
        P("pipe", "ctx", None),
        P("pipe", "ctx", None),
        P("pipe", "ctx", None),
        P("pipe", None, None),
    )
    return jax.shard_map(body, mesh=mesh, in_specs=in_specs, out_specs=out_specs, check_vma=False)
```

profile of v0, /device:TPU:120, one launch (start us, length us, event | category | flops | bytes accessed | tf_op | source)
XLA Modules:
  0.0 820.5 jit_solution(18369407955450212674)
XLA Ops:
  19.9 29.7 %all_gather.11 = s32[1,2048]{1,0:T(1,128)} all-gather(s32[1,128]{1,0:T(1,128)} %param.16), channel_id=1, replica_groups=mesh['pipe'=16,'ctx'=16] {'ctx'}, dimensions={1}, use_global_device_ids=true | all-gather | bytes 8704 | tf_op jit(solution)/shard_map/all_gather | solution.py:61
  61.2 21.9 %all-gather.4.cloned.1.call-done = bf16[2048,512]{1,0:T(8,128)(2,1)} async-done(((bf16[128,512]{1,0:T(8,128)(2,1)}), bf16[2048,512]{1,0:T(8,128)(2,1)}) %all-gather.4.cloned.1.call-update) | async-done | bytes 2097168 | tf_op jit(solution)/shard_map/all_gather | solution.py:84
  83.1 71.5 %all-gather.6.cloned.1.call-done = bf16[1,2048,512]{2,1,0:T(8,128)(2,1)} async-done(((bf16[1,128,512]{2,1,0:T(8,128)(2,1)}), bf16[1,2048,512]{2,1,0:T(8,128)(2,1)}) %all-gather.6.cloned.1.call-update) | async-done | bytes 2097168 | tf_op jit(solution)/shard_map/all_gather | solution.py:85
  154.6 59.0 %conditional.2 = (f32[128,4,8]{0,2,1:T(8,128)S(1)}, f32[128,4,8]{0,2,1:T(8,128)S(1)}, f32[128,4,8]{0,2,1:T(8,128)S(1)}, f32[128,4,8,128]{0,3,2,1:T(8,128)}) conditional(s32[]{:T(128)} %convert_element_type.134, () %tuple.47, (pred[128,1,1,2048]{0,3,2,1:T(8,128)(4,1)S(1)}, bf16[2048,512]{1,0:T(8,128)(2,1)}, bf16[128,4,8,128]{0,3,2,1:T(8,128)(2,1)S(1)}, ...), branch_computations={%region_3.0_spmd, %region_4.7_spmd} | conditional | flops 4404015104 | bytes 121766040 | solution.py:109
  154.6 4.0 reshape.335
  158.6 15.1 %fusion = (f32[128,4,8]{0,2,1:T(8,128)S(1)}, f32[4,2048,128,8]{2,1,3,0:T(8,128)}) fusion(pred[128,2048]{0,1:T(8,128)(4,1)S(1)} %bitcast.106, bf16[128,4,8,128]{0,3,2,1:T(8,128)(2,1)S(1)} %get-tuple-element.442, bf16[2048,4,128,1]{2,1,0,3:T(4,128)(2,1)} %bitcast.110), kind=kOutput, calls=%fused_computation.2 | convolution fusion | flops 2172645376 | bytes 36978688 | tf_op jit(solution)/shard_map/cond/branch_1_fun/qgrd,kgd->qgrk/dot_general | solution.py:95
  173.7 14.8 %fusion.2 = f32[128,4,8]{0,2,1:T(8,128)S(1)} fusion(f32[4,2048,128,8]{2,1,3,0:T(8,128)} %get-tuple-element.478, f32[128,4,8]{0,2,1:T(8,128)S(1)} %broadcast_maximum_fusion, pred[128,2048]{0,1:T(8,128)(4,1)S(1)} %bitcast.107), kind=kLoop, calls=%fused_computation.4 | loop fusion | flops 41938944 | bytes 33849344 | tf_op jit(solution)/shard_map/cond/branch_1_fun/reduce_sum | solution.py:100
  188.6 4.0 reshape.336
  192.5 18.2 %fusion.9 = f32[128,4,8,128]{3,0,2,1:T(8,128)} fusion(bf16[2048,4,128,1]{2,1,0,3:T(4,128)(2,1)} %bitcast.116, f32[4,2048,128,8]{2,1,3,0:T(8,128)} %get-tuple-element.478, f32[128,4,8]{0,2,1:T(8,128)S(1)} %broadcast_maximum_fusion, pred[128,2048]{0,1:T(8,128)(4,1)S(1)} %bitcast.108), kind=kOutput, calls=%fused_computation.10 | convolution fusion | flops 2189426688 | bytes 38027264 | tf_op jit(solution)/shard_map/cond/branch_1_fun/qgrk,kgd->qgrd/dot_general | solution.py:101
  219.3 516.9 %while.24 = (s32[]{:T(128)}, bf16[128,512]{1,0:T(8,128)(2,1)S(1)}, bf16[128,512]{1,0:T(8,128)(2,1)S(1)}, f32[128,512]{0,1:T(8,128)S(1)}, f32[128,512]{0,1:T(8,12...) while((s32[]{:T(128)}, bf16[128,512]{1,0:T(8,128)(2,1)S(1)}, ...), condition=%wide.region_12.13_spmd.clone, body=%wide.region_8.12_spmd.clone.sunk | while | flops 676446208 | bytes 26152600 | solution.py:162
  224.1 13.6 %conditional.5 = ((f32[128,4,8,128]{3,0,2,1:T(8,128)}, f32[128,512]{0,1:T(8,128)}, f32[128,512]{0,1:T(8,128)S(1)})) conditional(s32[]{:T(128)} %convert_element_type.184, (f32[128,4,8,128]{3,0,2,1:T(8,128)}, f32[128,512]{0,1:T(8,128)}, f32[128,512]{0,1:T(8,128)S(1)}) %tuple.91, (s32[128]{0:T(128)S(1)}, s32[1,128]{1,0:T(1,128)}, ...), branch_computations={%region_10.10_spmd, %region_11.11_spmd} | conditional | flops 676020224 | bytes 20907040 | solution.py:151
  234.2 3.5 bitcast_add_fusion
  254.1 17.2 %collective-permute-start.2 = (bf16[128,512]{0,1:T(8,128)(2,1)S(1)}, bf16[128,512]{0,1:T(8,128)(2,1)S(1)}, u32[]{:S(2)}, u32[]{:S(2)}) collective-permute-start(bf16[128,512]{0,1:T(8,128)(2,1)S(1)} %convert_element_type.185), channel_id=1, source_target_pairs={{0,1},{1,2},{2,3},{3,4},{4,5},{5,6},{6,7},{7,8},{8,9},{9,10},{10,1... | collective-permute-start | bytes 393224 | tf_op jit(solution)/shard_map/while/body/eval_jaxpr/ppermute | solution.py:18
  287.6 15.0 %collective-permute-start.3 = (bf16[128,512]{0,1:T(8,128)(2,1)S(1)}, bf16[128,512]{0,1:T(8,128)(2,1)S(1)}, u32[]{:S(2)}, u32[]{:S(2)}) collective-permute-start(bf16[128,512]{0,1:T(8,128)(2,1)S(1)} %convert_element_type.187), channel_id=1, source_target_pairs={{0,1},{1,2},{2,3},{3,4},{4,5},{5,6},{6,7},{7,8},{8,9},{9,10},{10,1... | collective-permute-start | bytes 393224 | tf_op jit(solution)/shard_map/while/body/eval_jaxpr/ppermute | solution.py:18
  319.7 15.0 %collective-permute-start = (bf16[128,512]{1,0:T(8,128)(2,1)}, bf16[128,512]{1,0:T(8,128)(2,1)S(1)}, u32[]{:S(2)}, u32[]{:S(2)}) collective-permute-start(bf16[128,512]{1,0:T(8,128)(2,1)} %copy.153), channel_id=1, source_target_pairs={{0,1},{1,2},{2,3},{3,4},{4,5},{5,6},{6,7},{7,8},{8,9},{9,10},{10,1... | collective-permute-start | bytes 393224 | tf_op jit(solution)/shard_map/while/body/eval_jaxpr/ppermute | solution.py:18
  344.7 13.6 %conditional.5 = ((f32[128,4,8,128]{3,0,2,1:T(8,128)}, f32[128,512]{0,1:T(8,128)}, f32[128,512]{0,1:T(8,128)S(1)})) conditional(s32[]{:T(128)} %convert_element_type.184, (f32[128,4,8,128]{3,0,2,1:T(8,128)}, f32[128,512]{0,1:T(8,128)}, f32[128,512]{0,1:T(8,128)S(1)}) %tuple.91, (s32[128]{0:T(128)S(1)}, s32[1,128]{1,0:T(1,128)}, ...), branch_computations={%region_10.10_spmd, %region_11.11_spmd} | conditional | flops 676020224 | bytes 20907040 | solution.py:151
  354.9 3.5 bitcast_add_fusion
  359.6 6.0 collective-permute-start
  375.5 13.6 %conditional.5 = ((f32[128,4,8,128]{3,0,2,1:T(8,128)}, f32[128,512]{0,1:T(8,128)}, f32[128,512]{0,1:T(8,128)S(1)})) conditional(s32[]{:T(128)} %convert_element_type.184, (f32[128,4,8,128]{3,0,2,1:T(8,128)}, f32[128,512]{0,1:T(8,128)}, f32[128,512]{0,1:T(8,128)S(1)}) %tuple.91, (s32[128]{0:T(128)S(1)}, s32[1,128]{1,0:T(1,128)}, ...), branch_computations={%region_10.10_spmd, %region_11.11_spmd} | conditional | flops 676020224 | bytes 20907040 | solution.py:151
  385.7 3.5 bitcast_add_fusion
  406.3 13.6 %conditional.5 = ((f32[128,4,8,128]{3,0,2,1:T(8,128)}, f32[128,512]{0,1:T(8,128)}, f32[128,512]{0,1:T(8,128)S(1)})) conditional(s32[]{:T(128)} %convert_element_type.184, (f32[128,4,8,128]{3,0,2,1:T(8,128)}, f32[128,512]{0,1:T(8,128)}, f32[128,512]{0,1:T(8,128)S(1)}) %tuple.91, (s32[128]{0:T(128)S(1)}, s32[1,128]{1,0:T(1,128)}, ...), branch_computations={%region_10.10_spmd, %region_11.11_spmd} | conditional | flops 676020224 | bytes 20907040 | solution.py:151
  416.5 3.5 bitcast_add_fusion
  437.1 13.6 %conditional.5 = ((f32[128,4,8,128]{3,0,2,1:T(8,128)}, f32[128,512]{0,1:T(8,128)}, f32[128,512]{0,1:T(8,128)S(1)})) conditional(s32[]{:T(128)} %convert_element_type.184, (f32[128,4,8,128]{3,0,2,1:T(8,128)}, f32[128,512]{0,1:T(8,128)}, f32[128,512]{0,1:T(8,128)S(1)}) %tuple.91, (s32[128]{0:T(128)S(1)}, s32[1,128]{1,0:T(1,128)}, ...), branch_computations={%region_10.10_spmd, %region_11.11_spmd} | conditional | flops 676020224 | bytes 20907040 | solution.py:151
  468.1 16.2 %collective-permute-start.2 = (bf16[128,512]{0,1:T(8,128)(2,1)S(1)}, bf16[128,512]{0,1:T(8,128)(2,1)S(1)}, u32[]{:S(2)}, u32[]{:S(2)}) collective-permute-start(bf16[128,512]{0,1:T(8,128)(2,1)S(1)} %convert_element_type.185), channel_id=1, source_target_pairs={{0,1},{1,2},{2,3},{3,4},{4,5},{5,6},{6,7},{7,8},{8,9},{9,10},{10,1... | collective-permute-start | bytes 393224 | tf_op jit(solution)/shard_map/while/body/eval_jaxpr/ppermute | solution.py:18
  497.4 13.6 %conditional.5 = ((f32[128,4,8,128]{3,0,2,1:T(8,128)}, f32[128,512]{0,1:T(8,128)}, f32[128,512]{0,1:T(8,128)S(1)})) conditional(s32[]{:T(128)} %convert_element_type.184, (f32[128,4,8,128]{3,0,2,1:T(8,128)}, f32[128,512]{0,1:T(8,128)}, f32[128,512]{0,1:T(8,128)S(1)}) %tuple.91, (s32[128]{0:T(128)S(1)}, s32[1,128]{1,0:T(1,128)}, ...), branch_computations={%region_10.10_spmd, %region_11.11_spmd} | conditional | flops 676020224 | bytes 20907040 | solution.py:151
  507.5 3.5 bitcast_add_fusion
  515.2 3.7 collective-permute-start
  529.4 13.6 %conditional.5 = ((f32[128,4,8,128]{3,0,2,1:T(8,128)}, f32[128,512]{0,1:T(8,128)}, f32[128,512]{0,1:T(8,128)S(1)})) conditional(s32[]{:T(128)} %convert_element_type.184, (f32[128,4,8,128]{3,0,2,1:T(8,128)}, f32[128,512]{0,1:T(8,128)}, f32[128,512]{0,1:T(8,128)S(1)}) %tuple.91, (s32[128]{0:T(128)S(1)}, s32[1,128]{1,0:T(1,128)}, ...), branch_computations={%region_10.10_spmd, %region_11.11_spmd} | conditional | flops 676020224 | bytes 20907040 | solution.py:151
  539.6 3.5 bitcast_add_fusion
  544.0 4.5 collective-permute-start.2
  548.7 7.1 collective-permute-start
  568.1 17.3 %collective-permute-start.2 = (bf16[128,512]{0,1:T(8,128)(2,1)S(1)}, bf16[128,512]{0,1:T(8,128)(2,1)S(1)}, u32[]{:S(2)}, u32[]{:S(2)}) collective-permute-start(bf16[128,512]{0,1:T(8,128)(2,1)S(1)} %convert_element_type.185), channel_id=1, source_target_pairs={{0,1},{1,2},{2,3},{3,4},{4,5},{5,6},{6,7},{7,8},{8,9},{9,10},{10,1... | collective-permute-start | bytes 393224 | tf_op jit(solution)/shard_map/while/body/eval_jaxpr/ppermute | solution.py:18
  605.3 13.6 %conditional.5 = ((f32[128,4,8,128]{3,0,2,1:T(8,128)}, f32[128,512]{0,1:T(8,128)}, f32[128,512]{0,1:T(8,128)S(1)})) conditional(s32[]{:T(128)} %convert_element_type.184, (f32[128,4,8,128]{3,0,2,1:T(8,128)}, f32[128,512]{0,1:T(8,128)}, f32[128,512]{0,1:T(8,128)S(1)}) %tuple.91, (s32[128]{0:T(128)S(1)}, s32[1,128]{1,0:T(1,128)}, ...), branch_computations={%region_10.10_spmd, %region_11.11_spmd} | conditional | flops 676020224 | bytes 20907040 | solution.py:151
  615.5 3.5 bitcast_add_fusion
  625.3 5.4 collective-permute-done.2
  643.4 13.6 %conditional.5 = ((f32[128,4,8,128]{3,0,2,1:T(8,128)}, f32[128,512]{0,1:T(8,128)}, f32[128,512]{0,1:T(8,128)S(1)})) conditional(s32[]{:T(128)} %convert_element_type.184, (f32[128,4,8,128]{3,0,2,1:T(8,128)}, f32[128,512]{0,1:T(8,128)}, f32[128,512]{0,1:T(8,128)S(1)}) %tuple.91, (s32[128]{0:T(128)S(1)}, s32[1,128]{1,0:T(1,128)}, ...), branch_computations={%region_10.10_spmd, %region_11.11_spmd} | conditional | flops 676020224 | bytes 20907040 | solution.py:151
  653.5 3.5 bitcast_add_fusion
  661.8 4.5 collective-permute-done.2
  678.1 13.6 %conditional.5 = ((f32[128,4,8,128]{3,0,2,1:T(8,128)}, f32[128,512]{0,1:T(8,128)}, f32[128,512]{0,1:T(8,128)S(1)})) conditional(s32[]{:T(128)} %convert_element_type.184, (f32[128,4,8,128]{3,0,2,1:T(8,128)}, f32[128,512]{0,1:T(8,128)}, f32[128,512]{0,1:T(8,128)S(1)}) %tuple.91, (s32[128]{0:T(128)S(1)}, s32[1,128]{1,0:T(1,128)}, ...), branch_computations={%region_10.10_spmd, %region_11.11_spmd} | conditional | flops 676020224 | bytes 20907040 | solution.py:151
  688.2 3.5 bitcast_add_fusion
  695.2 5.1 collective-permute-done.2
  711.0 13.6 %conditional.5 = ((f32[128,4,8,128]{3,0,2,1:T(8,128)}, f32[128,512]{0,1:T(8,128)}, f32[128,512]{0,1:T(8,128)S(1)})) conditional(s32[]{:T(128)} %convert_element_type.184, (f32[128,4,8,128]{3,0,2,1:T(8,128)}, f32[128,512]{0,1:T(8,128)}, f32[128,512]{0,1:T(8,128)S(1)}) %tuple.91, (s32[128]{0:T(128)S(1)}, s32[1,128]{1,0:T(1,128)}, ...), branch_computations={%region_10.10_spmd, %region_11.11_spmd} | conditional | flops 676020224 | bytes 20907040 | solution.py:151
  721.2 3.5 bitcast_add_fusion
  726.5 5.4 collective-permute-done.2
  755.5 4.6 multiply_reduce_fusion
  760.1 38.1 %psum.7 = f32[2,128]{1,0:T(2,128)S(1)} all-reduce(f32[2,128]{1,0:T(2,128)S(1)} %pad_maximum_fusion.4), channel_id=1, replica_groups=mesh['pipe'=16,'ctx'=16] {'ctx'}, use_global_device_ids=true, to_apply=%region_19.20 | all-reduce | flops 256 | bytes 2048 | tf_op jit(solution)/shard_map/psum | solution.py:180
  799.4 3.6 collective-permute-done.5
  803.0 5.1 collective-permute-done.6
  (481 shorter events, 406.5 us)
Async XLA Ops:
  7.2 75.9 %all-gather.4.cloned.1.call-start = ((), (), s32[]{:S(2)}) async-start(), calls=%async_computation | async-start | bytes 2228224 | tf_op jit(solution)/shard_map/all_gather | solution.py:84
  13.3 141.4 %all-gather.6.cloned.1.call-start = ((), (), s32[]{:S(2)}) async-start(), calls=%async_computation.1 | async-start | bytes 2228224 | tf_op jit(solution)/shard_map/all_gather | solution.py:85
  238.7 6.7 collective-permute-start.2
  254.1 20.3 %collective-permute-start.2 = (bf16[128,512]{0,1:T(8,128)(2,1)S(1)}, bf16[128,512]{0,1:T(8,128)(2,1)S(1)}, u32[]{:S(2)}, u32[]{:S(2)}) collective-permute-start(bf16[128,512]{0,1:T(8,128)(2,1)S(1)} %convert_element_type.185), channel_id=1, source_target_pairs={{0,1},{1,2},{2,3},{3,4},{4,5},{5,6},{6,7},{7,8},{8,9},{9,10},{10,1... | collective-permute-start | bytes 393224 | tf_op jit(solution)/shard_map/while/body/eval_jaxpr/ppermute | solution.py:18
  273.2 6.0 collective-permute-start.1
  284.9 20.2 %collective-permute-start.2 = (bf16[128,512]{0,1:T(8,128)(2,1)S(1)}, bf16[128,512]{0,1:T(8,128)(2,1)S(1)}, u32[]{:S(2)}, u32[]{:S(2)}) collective-permute-start(bf16[128,512]{0,1:T(8,128)(2,1)S(1)} %convert_element_type.185), channel_id=1, source_target_pairs={{0,1},{1,2},{2,3},{3,4},{4,5},{5,6},{6,7},{7,8},{8,9},{9,10},{10,1... | collective-permute-start | bytes 393224 | tf_op jit(solution)/shard_map/while/body/eval_jaxpr/ppermute | solution.py:18
  287.6 17.6 %collective-permute-start.3 = (bf16[128,512]{0,1:T(8,128)(2,1)S(1)}, bf16[128,512]{0,1:T(8,128)(2,1)S(1)}, u32[]{:S(2)}, u32[]{:S(2)}) collective-permute-start(bf16[128,512]{0,1:T(8,128)(2,1)S(1)} %convert_element_type.187), channel_id=1, source_target_pairs={{0,1},{1,2},{2,3},{3,4},{4,5},{5,6},{6,7},{7,8},{8,9},{9,10},{10,1... | collective-permute-start | bytes 393224 | tf_op jit(solution)/shard_map/while/body/eval_jaxpr/ppermute | solution.py:18
  314.9 21.0 %collective-permute-start.2 = (bf16[128,512]{0,1:T(8,128)(2,1)S(1)}, bf16[128,512]{0,1:T(8,128)(2,1)S(1)}, u32[]{:S(2)}, u32[]{:S(2)}) collective-permute-start(bf16[128,512]{0,1:T(8,128)(2,1)S(1)} %convert_element_type.185), channel_id=1, source_target_pairs={{0,1},{1,2},{2,3},{3,4},{4,5},{5,6},{6,7},{7,8},{8,9},{9,10},{10,1... | collective-permute-start | bytes 393224 | tf_op jit(solution)/shard_map/while/body/eval_jaxpr/ppermute | solution.py:18
  317.6 18.3 %collective-permute-start.3 = (bf16[128,512]{0,1:T(8,128)(2,1)S(1)}, bf16[128,512]{0,1:T(8,128)(2,1)S(1)}, u32[]{:S(2)}, u32[]{:S(2)}) collective-permute-start(bf16[128,512]{0,1:T(8,128)(2,1)S(1)} %convert_element_type.187), channel_id=1, source_target_pairs={{0,1},{1,2},{2,3},{3,4},{4,5},{5,6},{6,7},{7,8},{8,9},{9,10},{10,1... | collective-permute-start | bytes 393224 | tf_op jit(solution)/shard_map/while/body/eval_jaxpr/ppermute | solution.py:18
  319.7 17.9 %collective-permute-start = (bf16[128,512]{1,0:T(8,128)(2,1)}, bf16[128,512]{1,0:T(8,128)(2,1)S(1)}, u32[]{:S(2)}, u32[]{:S(2)}) collective-permute-start(bf16[128,512]{1,0:T(8,128)(2,1)} %copy.153), channel_id=1, source_target_pairs={{0,1},{1,2},{2,3},{3,4},{4,5},{5,6},{6,7},{7,8},{8,9},{9,10},{10,1... | collective-permute-start | bytes 393224 | tf_op jit(solution)/shard_map/while/body/eval_jaxpr/ppermute | solution.py:18
  359.4 7.4 collective-permute-start.2
  359.5 7.3 collective-permute-start.3
  359.6 8.8 %collective-permute-start = (bf16[128,512]{1,0:T(8,128)(2,1)}, bf16[128,512]{1,0:T(8,128)(2,1)S(1)}, u32[]{:S(2)}, u32[]{:S(2)}) collective-permute-start(bf16[128,512]{1,0:T(8,128)(2,1)} %copy.153), channel_id=1, source_target_pairs={{0,1},{1,2},{2,3},{3,4},{4,5},{5,6},{6,7},{7,8},{8,9},{9,10},{10,1... | collective-permute-start | bytes 393224 | tf_op jit(solution)/shard_map/while/body/eval_jaxpr/ppermute | solution.py:18
  390.2 6.3 collective-permute-start.2
  393.0 6.4 collective-permute-start
  420.9 6.3 collective-permute-start.2
  454.5 6.4 collective-permute-start
  455.8 6.5 collective-permute-start.1
  468.1 19.7 %collective-permute-start.2 = (bf16[128,512]{0,1:T(8,128)(2,1)S(1)}, bf16[128,512]{0,1:T(8,128)(2,1)S(1)}, u32[]{:S(2)}, u32[]{:S(2)}) collective-permute-start(bf16[128,512]{0,1:T(8,128)(2,1)S(1)} %convert_element_type.185), channel_id=1, source_target_pairs={{0,1},{1,2},{2,3},{3,4},{4,5},{5,6},{6,7},{7,8},{8,9},{9,10},{10,1... | collective-permute-start | bytes 393224 | tf_op jit(solution)/shard_map/while/body/eval_jaxpr/ppermute | solution.py:18
  484.5 6.7 collective-permute-start
  484.6 8.0 collective-permute-start.1
  512.0 9.8 %collective-permute-start.2 = (bf16[128,512]{0,1:T(8,128)(2,1)S(1)}, bf16[128,512]{0,1:T(8,128)(2,1)S(1)}, u32[]{:S(2)}, u32[]{:S(2)}) collective-permute-start(bf16[128,512]{0,1:T(8,128)(2,1)S(1)} %convert_element_type.185), channel_id=1, source_target_pairs={{0,1},{1,2},{2,3},{3,4},{4,5},{5,6},{6,7},{7,8},{8,9},{9,10},{10,1... | collective-permute-start | bytes 393224 | tf_op jit(solution)/shard_map/while/body/eval_jaxpr/ppermute | solution.py:18
  512.1 9.7 %collective-permute-start.3 = (bf16[128,512]{0,1:T(8,128)(2,1)S(1)}, bf16[128,512]{0,1:T(8,128)(2,1)S(1)}, u32[]{:S(2)}, u32[]{:S(2)}) collective-permute-start(bf16[128,512]{0,1:T(8,128)(2,1)S(1)} %convert_element_type.187), channel_id=1, source_target_pairs={{0,1},{1,2},{2,3},{3,4},{4,5},{5,6},{6,7},{7,8},{8,9},{9,10},{10,1... | collective-permute-start | bytes 393224 | tf_op jit(solution)/shard_map/while/body/eval_jaxpr/ppermute | solution.py:18
  515.2 8.0 collective-permute-start
  544.0 14.1 %collective-permute-start.2 = (bf16[128,512]{0,1:T(8,128)(2,1)S(1)}, bf16[128,512]{0,1:T(8,128)(2,1)S(1)}, u32[]{:S(2)}, u32[]{:S(2)}) collective-permute-start(bf16[128,512]{0,1:T(8,128)(2,1)S(1)} %convert_element_type.185), channel_id=1, source_target_pairs={{0,1},{1,2},{2,3},{3,4},{4,5},{5,6},{6,7},{7,8},{8,9},{9,10},{10,1... | collective-permute-start | bytes 393224 | tf_op jit(solution)/shard_map/while/body/eval_jaxpr/ppermute | solution.py:18
  548.6 9.6 %collective-permute-start.3 = (bf16[128,512]{0,1:T(8,128)(2,1)S(1)}, bf16[128,512]{0,1:T(8,128)(2,1)S(1)}, u32[]{:S(2)}, u32[]{:S(2)}) collective-permute-start(bf16[128,512]{0,1:T(8,128)(2,1)S(1)} %convert_element_type.187), channel_id=1, source_target_pairs={{0,1},{1,2},{2,3},{3,4},{4,5},{5,6},{6,7},{7,8},{8,9},{9,10},{10,1... | collective-permute-start | bytes 393224 | tf_op jit(solution)/shard_map/while/body/eval_jaxpr/ppermute | solution.py:18
  548.7 10.1 %collective-permute-start = (bf16[128,512]{1,0:T(8,128)(2,1)}, bf16[128,512]{1,0:T(8,128)(2,1)S(1)}, u32[]{:S(2)}, u32[]{:S(2)}) collective-permute-start(bf16[128,512]{1,0:T(8,128)(2,1)} %copy.153), channel_id=1, source_target_pairs={{0,1},{1,2},{2,3},{3,4},{4,5},{5,6},{6,7},{7,8},{8,9},{9,10},{10,1... | collective-permute-start | bytes 393224 | tf_op jit(solution)/shard_map/while/body/eval_jaxpr/ppermute | solution.py:18
  555.8 6.5 collective-permute-start.1
  568.1 25.3 %collective-permute-start.2 = (bf16[128,512]{0,1:T(8,128)(2,1)S(1)}, bf16[128,512]{0,1:T(8,128)(2,1)S(1)}, u32[]{:S(2)}, u32[]{:S(2)}) collective-permute-start(bf16[128,512]{0,1:T(8,128)(2,1)S(1)} %convert_element_type.185), channel_id=1, source_target_pairs={{0,1},{1,2},{2,3},{3,4},{4,5},{5,6},{6,7},{7,8},{8,9},{9,10},{10,1... | collective-permute-start | bytes 393224 | tf_op jit(solution)/shard_map/while/body/eval_jaxpr/ppermute | solution.py:18
  585.4 10.8 %collective-permute-start.3 = (bf16[128,512]{0,1:T(8,128)(2,1)S(1)}, bf16[128,512]{0,1:T(8,128)(2,1)S(1)}, u32[]{:S(2)}, u32[]{:S(2)}) collective-permute-start(bf16[128,512]{0,1:T(8,128)(2,1)S(1)} %convert_element_type.187), channel_id=1, source_target_pairs={{0,1},{1,2},{2,3},{3,4},{4,5},{5,6},{6,7},{7,8},{8,9},{9,10},{10,1... | collective-permute-start | bytes 393224 | tf_op jit(solution)/shard_map/while/body/eval_jaxpr/ppermute | solution.py:18
  587.6 11.3 %collective-permute-start = (bf16[128,512]{1,0:T(8,128)(2,1)}, bf16[128,512]{1,0:T(8,128)(2,1)S(1)}, u32[]{:S(2)}, u32[]{:S(2)}) collective-permute-start(bf16[128,512]{1,0:T(8,128)(2,1)} %copy.153), channel_id=1, source_target_pairs={{0,1},{1,2},{2,3},{3,4},{4,5},{5,6},{6,7},{7,8},{8,9},{9,10},{10,1... | collective-permute-start | bytes 393224 | tf_op jit(solution)/shard_map/while/body/eval_jaxpr/ppermute | solution.py:18
  590.2 10.3 %collective-permute-start.1 = (bf16[128,512]{1,0:T(8,128)(2,1)}, bf16[128,512]{1,0:T(8,128)(2,1)S(1)}, u32[]{:S(2)}, u32[]{:S(2)}) collective-permute-start(bf16[128,512]{1,0:T(8,128)(2,1)} %copy.154), channel_id=1, source_target_pairs={{0,1},{1,2},{2,3},{3,4},{4,5},{5,6},{6,7},{7,8},{8,9},{9,10},{10,1... | collective-permute-start | bytes 393224 | tf_op jit(solution)/shard_map/while/body/eval_jaxpr/ppermute | solution.py:18
  620.0 10.8 %collective-permute-start.2 = (bf16[128,512]{0,1:T(8,128)(2,1)S(1)}, bf16[128,512]{0,1:T(8,128)(2,1)S(1)}, u32[]{:S(2)}, u32[]{:S(2)}) collective-permute-start(bf16[128,512]{0,1:T(8,128)(2,1)S(1)} %convert_element_type.185), channel_id=1, source_target_pairs={{0,1},{1,2},{2,3},{3,4},{4,5},{5,6},{6,7},{7,8},{8,9},{9,10},{10,1... | collective-permute-start | bytes 393224 | tf_op jit(solution)/shard_map/while/body/eval_jaxpr/ppermute | solution.py:18
  620.1 13.4 %collective-permute-start.3 = (bf16[128,512]{0,1:T(8,128)(2,1)S(1)}, bf16[128,512]{0,1:T(8,128)(2,1)S(1)}, u32[]{:S(2)}, u32[]{:S(2)}) collective-permute-start(bf16[128,512]{0,1:T(8,128)(2,1)S(1)} %convert_element_type.187), channel_id=1, source_target_pairs={{0,1},{1,2},{2,3},{3,4},{4,5},{5,6},{6,7},{7,8},{8,9},{9,10},{10,1... | collective-permute-start | bytes 393224 | tf_op jit(solution)/shard_map/while/body/eval_jaxpr/ppermute | solution.py:18
  622.8 13.5 %collective-permute-start = (bf16[128,512]{1,0:T(8,128)(2,1)}, bf16[128,512]{1,0:T(8,128)(2,1)S(1)}, u32[]{:S(2)}, u32[]{:S(2)}) collective-permute-start(bf16[128,512]{1,0:T(8,128)(2,1)} %copy.153), channel_id=1, source_target_pairs={{0,1},{1,2},{2,3},{3,4},{4,5},{5,6},{6,7},{7,8},{8,9},{9,10},{10,1... | collective-permute-start | bytes 393224 | tf_op jit(solution)/shard_map/while/body/eval_jaxpr/ppermute | solution.py:18
  625.2 13.3 %collective-permute-start.1 = (bf16[128,512]{1,0:T(8,128)(2,1)}, bf16[128,512]{1,0:T(8,128)(2,1)S(1)}, u32[]{:S(2)}, u32[]{:S(2)}) collective-permute-start(bf16[128,512]{1,0:T(8,128)(2,1)} %copy.154), channel_id=1, source_target_pairs={{0,1},{1,2},{2,3},{3,4},{4,5},{5,6},{6,7},{7,8},{8,9},{9,10},{10,1... | collective-permute-start | bytes 393224 | tf_op jit(solution)/shard_map/while/body/eval_jaxpr/ppermute | solution.py:18
  658.0 8.4 %collective-permute-start.2 = (bf16[128,512]{0,1:T(8,128)(2,1)S(1)}, bf16[128,512]{0,1:T(8,128)(2,1)S(1)}, u32[]{:S(2)}, u32[]{:S(2)}) collective-permute-start(bf16[128,512]{0,1:T(8,128)(2,1)S(1)} %convert_element_type.185), channel_id=1, source_target_pairs={{0,1},{1,2},{2,3},{3,4},{4,5},{5,6},{6,7},{7,8},{8,9},{9,10},{10,1... | collective-permute-start | bytes 393224 | tf_op jit(solution)/shard_map/while/body/eval_jaxpr/ppermute | solution.py:18
  658.1 11.1 %collective-permute-start.3 = (bf16[128,512]{0,1:T(8,128)(2,1)S(1)}, bf16[128,512]{0,1:T(8,128)(2,1)S(1)}, u32[]{:S(2)}, u32[]{:S(2)}) collective-permute-start(bf16[128,512]{0,1:T(8,128)(2,1)S(1)} %convert_element_type.187), channel_id=1, source_target_pairs={{0,1},{1,2},{2,3},{3,4},{4,5},{5,6},{6,7},{7,8},{8,9},{9,10},{10,1... | collective-permute-start | bytes 393224 | tf_op jit(solution)/shard_map/while/body/eval_jaxpr/ppermute | solution.py:18
  658.2 13.7 %collective-permute-start = (bf16[128,512]{1,0:T(8,128)(2,1)}, bf16[128,512]{1,0:T(8,128)(2,1)S(1)}, u32[]{:S(2)}, u32[]{:S(2)}) collective-permute-start(bf16[128,512]{1,0:T(8,128)(2,1)} %copy.153), channel_id=1, source_target_pairs={{0,1},{1,2},{2,3},{3,4},{4,5},{5,6},{6,7},{7,8},{8,9},{9,10},{10,1... | collective-permute-start | bytes 393224 | tf_op jit(solution)/shard_map/while/body/eval_jaxpr/ppermute | solution.py:18
  659.5 13.7 %collective-permute-start.1 = (bf16[128,512]{1,0:T(8,128)(2,1)}, bf16[128,512]{1,0:T(8,128)(2,1)S(1)}, u32[]{:S(2)}, u32[]{:S(2)}) collective-permute-start(bf16[128,512]{1,0:T(8,128)(2,1)} %copy.154), channel_id=1, source_target_pairs={{0,1},{1,2},{2,3},{3,4},{4,5},{5,6},{6,7},{7,8},{8,9},{9,10},{10,1... | collective-permute-start | bytes 393224 | tf_op jit(solution)/shard_map/while/body/eval_jaxpr/ppermute | solution.py:18
  692.7 7.7 collective-permute-start.2
  692.8 10.3 %collective-permute-start.3 = (bf16[128,512]{0,1:T(8,128)(2,1)S(1)}, bf16[128,512]{0,1:T(8,128)(2,1)S(1)}, u32[]{:S(2)}, u32[]{:S(2)}) collective-permute-start(bf16[128,512]{0,1:T(8,128)(2,1)S(1)} %convert_element_type.187), channel_id=1, source_target_pairs={{0,1},{1,2},{2,3},{3,4},{4,5},{5,6},{6,7},{7,8},{8,9},{9,10},{10,1... | collective-permute-start | bytes 393224 | tf_op jit(solution)/shard_map/while/body/eval_jaxpr/ppermute | solution.py:18
  692.9 11.9 %collective-permute-start = (bf16[128,512]{1,0:T(8,128)(2,1)}, bf16[128,512]{1,0:T(8,128)(2,1)S(1)}, u32[]{:S(2)}, u32[]{:S(2)}) collective-permute-start(bf16[128,512]{1,0:T(8,128)(2,1)} %copy.153), channel_id=1, source_target_pairs={{0,1},{1,2},{2,3},{3,4},{4,5},{5,6},{6,7},{7,8},{8,9},{9,10},{10,1... | collective-permute-start | bytes 393224 | tf_op jit(solution)/shard_map/while/body/eval_jaxpr/ppermute | solution.py:18
  693.0 13.3 %collective-permute-start.1 = (bf16[128,512]{1,0:T(8,128)(2,1)}, bf16[128,512]{1,0:T(8,128)(2,1)S(1)}, u32[]{:S(2)}, u32[]{:S(2)}) collective-permute-start(bf16[128,512]{1,0:T(8,128)(2,1)} %copy.154), channel_id=1, source_target_pairs={{0,1},{1,2},{2,3},{3,4},{4,5},{5,6},{6,7},{7,8},{8,9},{9,10},{10,1... | collective-permute-start | bytes 393224 | tf_op jit(solution)/shard_map/while/body/eval_jaxpr/ppermute | solution.py:18
  725.7 6.2 collective-permute-start.2
  726.2 7.1 collective-permute-start.3
  726.3 8.4 %collective-permute-start = (bf16[128,512]{1,0:T(8,128)(2,1)}, bf16[128,512]{1,0:T(8,128)(2,1)S(1)}, u32[]{:S(2)}, u32[]{:S(2)}) collective-permute-start(bf16[128,512]{1,0:T(8,128)(2,1)} %copy.153), channel_id=1, source_target_pairs={{0,1},{1,2},{2,3},{3,4},{4,5},{5,6},{6,7},{7,8},{8,9},{9,10},{10,1... | collective-permute-start | bytes 393224 | tf_op jit(solution)/shard_map/while/body/eval_jaxpr/ppermute | solution.py:18
  726.4 9.8 %collective-permute-start.1 = (bf16[128,512]{1,0:T(8,128)(2,1)}, bf16[128,512]{1,0:T(8,128)(2,1)S(1)}, u32[]{:S(2)}, u32[]{:S(2)}) collective-permute-start(bf16[128,512]{1,0:T(8,128)(2,1)} %copy.154), channel_id=1, source_target_pairs={{0,1},{1,2},{2,3},{3,4},{4,5},{5,6},{6,7},{7,8},{8,9},{9,10},{10,1... | collective-permute-start | bytes 393224 | tf_op jit(solution)/shard_map/while/body/eval_jaxpr/ppermute | solution.py:18
  (51 other events, 431.2 us)
Sparse Core Ops, SparseCore 0:
  13.4 69.6 all-gather.3
  85.5 69.1 all-gather.5
where the time goes:
time: 829 us; the launch traced here: 821 us
  waiting for transfers between devices  208 us (25%)
  starting transfers between devices  172 us (21%)
  matrix products  128 us (15%)
  other arithmetic  116 us (14%)
  local copies, waits for them, and re-layouts  103 us (12%)
  blocking collectives  67.8 us (8%)
  between operations  15.1 us (2%)
  loops' own time  11 us (1%)
    ppermute x64, starting transfers between devices, from_behind(): lax.ppermute(array, axis, [(i, (i + by) % devices) for i in range(devices)])  172 us
    ppermute x64, waiting for transfers between devices, from_behind(): lax.ppermute(array, axis, [(i, (i + by) % devices) for i in range(devices)])  101 us
    all_gather x1, waiting for transfers between devices, body(): v_piece = lax.all_gather(values, 'ctx', axis=0, tiled=True)  71.5 us
    dot_general x11, matrix products, grad_tile(): jnp.einsum('qgrk,kgd->qgrd', d_score, k_head, preferred_element_type=jnp....  38.3 us
    psum x1, blocking collectives, body(): summed = lax.psum(own, 'ctx')  38.1 us
    all_gather x1, blocking collectives, body(): every_pos = lax.all_gather(positions, 'ctx', axis=1, tiled=True)[0]  29.7 us
    reduce_or x16, other arithmetic, cycle_step(): jnp.any(visible(key_pos))  22.3 us
    all_gather x1, waiting for transfers between devices, body(): k_piece = lax.all_gather(k_rot, 'ctx', axis=0, tiled=True)  21.9 us
  transfers between devices with their start and end apart: 70, of which 55 were waited for; matrix products, arithmetic and copies ran while one was open for 2% of the time, Pallas kernels for 0%

commit v1 on v0

v1 whole, which is shorter than its diff:
```python
import functools

import jax
import jax.numpy as jnp
import numpy as np
from jax import lax
from jax.experimental import pallas as pl
from jax.experimental.pallas import tpu as pltpu
from jax.sharding import PartitionSpec as P

HQ = 32
HK = 4
DH = 128
THETA = 1000000.0
EPS = 1e-06
NEG = -1e30

TOK = 128
RUN = 64
SEQ = 2048
PAD = 16
GROUP = 8
QROWS = RUN * GROUP
KB = 256
NKB = SEQ // KB
HALF = HQ * DH // 2
SCALE = DH**-0.5
SCALE2 = SCALE * 1.4426950408889634
SHARDS = 16


def rope_table():
    freq = (THETA ** (-(np.arange(DH // 2, dtype=np.float64) * 2.0) / DH)).astype(np.float32)
    turn = np.arange(SEQ, dtype=np.float32)[:, None] * freq[None, :]
    turn = turn.astype(np.float64)
    return np.concatenate([np.cos(turn), np.sin(turn)], -1).astype(np.float32)


def dot(a, b, dims=((1,), (0,))):
    return lax.dot_general(a, b, (dims, ((), ())), preferred_element_type=jnp.float32)


NT = ((1,), (1,))


def cos_sin(tab):
    low = lax.broadcasted_iota(jnp.int32, tab.shape, 1) < DH // 2
    other = pltpu.roll(tab, DH // 2, 1)
    return jnp.where(low, tab, other), jnp.where(low, -other, tab)


def turn_by(x, cosine, sine):
    return x * cosine + pltpu.roll(x, DH // 2, 1) * sine


def turn_back(x, cosine, sine):
    return x * cosine - pltpu.roll(x, DH // 2, 1) * sine


def prep_kernel(pos, side, key, value, tab, gains, mine, other):
    run = pl.program_id(0)
    cosine, sine = cos_sin(tab[...])
    gain = gains[0, 1:2, :]
    pieces = []
    for head in range(HK):
        x = key[0, :, head * DH : (head + 1) * DH].astype(jnp.float32)
        inverse = lax.rsqrt(jnp.mean(x * x, -1, keepdims=True) + EPS)
        pieces.append(turn_by(x * inverse * gain, cosine, sine).astype(jnp.bfloat16))
    v = value[0]
    first = jnp.concatenate(pieces[:2] + [v[:, : 2 * DH]], -1)
    second = jnp.concatenate(pieces[2:] + [v[:, 2 * DH :]], -1)
    upper = side[0] == 1
    rows = pl.ds(pl.multiple_of(run * RUN, RUN), RUN)
    mine[rows, :] = jnp.where(upper, second, first)
    other[rows, :] = jnp.where(upper, first, second)

    @pl.when(run == 0)
    def _():
        lane = lax.broadcasted_iota(jnp.int32, (PAD, 4 * DH), 1)
        a = (pos[0, 0] // RUN).astype(jnp.float32)
        b = (pos[0, RUN] // RUN).astype(jnp.float32)
        tail = jnp.where(lane == 0, a, jnp.where(lane == 1, b, 0.0)).astype(jnp.bfloat16)
        mine[TOK:, :] = tail
        other[TOK:, :] = tail


def prep(positions, side, key, value, tab, gains):
    block = jax.ShapeDtypeStruct((TOK + PAD, 4 * DH), jnp.bfloat16)
    whole = pl.BlockSpec((TOK + PAD, 4 * DH), lambda r, p, s: (0, 0))
    return pl.pallas_call(
        prep_kernel,
        out_shape=(block, block),
        grid_spec=pltpu.PrefetchScalarGridSpec(
            num_scalar_prefetch=2,
            grid=(2,),
            in_specs=[
                pl.BlockSpec((1, RUN, HK * DH), lambda r, p, s: (0, r, 0)),
                pl.BlockSpec((1, RUN, HK * DH), lambda r, p, s: (0, r, 0)),
                pl.BlockSpec((RUN, DH), lambda r, p, s: (p[0, r * RUN] // RUN, 0)),
                pl.BlockSpec((1, 2, DH), lambda r, p, s: (0, 0, 0)),
            ],
            out_specs=(whole, whole),
        ),
        name="prep",
    )(positions, side, key, value, tab, gains)


def attention_kernel(blk, side, *refs):
    q_own, q_far, g_own, g_far, tab, gains = refs[:6]
    shards = refs[6 : 6 + SHARDS]
    att_own, att_far, dq_own, dq_far = refs[6 + SHARDS : 10 + SHARDS]
    outs = refs[10 + SHARDS : 10 + 2 * SHARDS]
    (own_out, ks, vs, kt, vt, scores, probs, dk, dv, o_acc, dq_acc, own_q, own_k) = refs[10 + 2 * SHARDS :]
    head = pl.program_id(0)
    run = pl.program_id(1)

    @pl.when(run == 0)
    def _():
        for a in range(SHARDS):
            k_all = jnp.where(head == 0, shards[a][:TOK, :DH], shards[a][:TOK, DH : 2 * DH])
            v_all = jnp.where(head == 0, shards[a][:TOK, 2 * DH : 3 * DH], shards[a][:TOK, 3 * DH :])
            for b in range(2):
                to = pl.ds(pl.multiple_of(blk[2 * a + b] * RUN, RUN), RUN)
                ks[to, :] = k_all[b * RUN : (b + 1) * RUN]
                vs[to, :] = v_all[b * RUN : (b + 1) * RUN]
        for j in range(NKB):
            kt[j] = ks[j * KB : (j + 1) * KB, :].T
            vt[j] = vs[j * KB : (j + 1) * KB, :].T
        dk[...] = jnp.zeros_like(dk)
        dv[...] = jnp.zeros_like(dv)

    @pl.when((run == 0) & (head == 0))
    def _():
        own_q[...] = jnp.zeros_like(own_q)
        own_k[...] = jnp.zeros_like(own_k)

    own = run < 2

    def stacked(near, far):
        x = jnp.where(own, near[0], far[...])
        return jnp.concatenate([x[:, h * DH : (h + 1) * DH] for h in range(GROUP)], 0)

    number = blk[run]
    cosine, sine = cos_sin(tab[pl.ds(pl.multiple_of(number * RUN, RUN), RUN), :])
    cosine = jnp.concatenate([cosine] * GROUP, 0)
    sine = jnp.concatenate([sine] * GROUP, 0)
    gain = gains[0, 0:1, :]
    x = stacked(q_own, q_far).astype(jnp.float32)
    q_inverse = lax.rsqrt(jnp.mean(x * x, -1, keepdims=True) + EPS)
    q_normed = x * q_inverse
    q_rot = turn_by(q_normed * gain, cosine, sine).astype(jnp.bfloat16)
    q_t = q_rot.T
    g_t = stacked(g_own, g_far).T

    last = number // (KB // RUN)
    lane = lax.broadcasted_iota(jnp.int32, (KB, QROWS), 1)
    row = lax.broadcasted_iota(jnp.int32, (KB, QROWS), 0)
    seen = row + last * KB <= number * RUN + (lane & (RUN - 1))

    def at(j):
        return pl.ds(pl.multiple_of(j * KB, KB), KB)

    def score(j):
        return dot(ks[at(j), :], q_t) * SCALE2

    def fold(x, op):
        return op(x.reshape(KB // 8, 8, QROWS), 0)

    s = jnp.where(seen, score(last), NEG)
    scores[at(last), :] = s

    def pass_a(j, top):
        s = score(j)
        scores[at(j), :] = s
        return jnp.maximum(top, fold(s, jnp.max))

    top = lax.fori_loop(0, last, pass_a, fold(s, jnp.max))
    top = jnp.max(top, 0, keepdims=True)

    o_acc[...] = jnp.zeros_like(o_acc)

    def pass_b(j, total):
        expo = jnp.exp2(scores[at(j), :] - top)
        low = expo.astype(jnp.bfloat16)
        probs[at(j), :] = low
        o_acc[...] += dot(vt[j], low)
        return total + fold(expo, jnp.sum)

    total = lax.fori_loop(0, last + 1, pass_b, jnp.zeros((8, QROWS), jnp.float32))
    inverse = 1.0 / jnp.sum(total, 0, keepdims=True)
    att_t = (o_acc[...] * inverse).astype(jnp.bfloat16)
    g_low = (g_t.astype(jnp.float32) * inverse).astype(jnp.bfloat16)
    delta = jnp.sum(g_low.astype(jnp.float32) * att_t.astype(jnp.float32), 0, keepdims=True)

    def unstacked(x):
        return jnp.concatenate([x[h * RUN : (h + 1) * RUN] for h in range(GROUP)], 1)

    att = unstacked(att_t.T)

    dq_acc[...] = jnp.zeros_like(dq_acc)

    def pass_c(j, carry):
        p = probs[at(j), :]
        d_prob = dot(vs[at(j), :], g_low)
        d_score = (p.astype(jnp.float32) * (d_prob - delta)).astype(jnp.bfloat16)
        dv[at(j), :] += dot(p, g_low, NT)
        dk[at(j), :] += dot(d_score, q_t, NT)
        dq_acc[...] += dot(kt[j], d_score)
        return carry

    lax.fori_loop(0, last + 1, pass_c, 0)

    dq_scaled = turn_back((dq_acc[...] * SCALE).T, cosine, sine)
    product = dq_scaled * q_normed
    own_q[...] += jnp.sum(product.reshape(QROWS // 8, 8, DH), 0)
    grad_normed = dq_scaled * gain
    inner = jnp.mean(grad_normed * q_normed, -1, keepdims=True)
    dq = unstacked((q_inverse * (grad_normed - q_normed * inner)).astype(jnp.bfloat16))

    @pl.when(own)
    def _():
        att_own[...] = att
        dq_own[...] = dq

    @pl.when(jnp.logical_not(own))
    def _():
        att_far[...] = att
        dq_far[...] = dq

    def write(column):
        for a in range(SHARDS):
            for b in range(2):
                src = pl.ds(pl.multiple_of(blk[2 * a + b] * RUN, RUN), RUN)
                rows = slice(b * RUN, (b + 1) * RUN)
                outs[a][rows, column * DH : (column + 1) * DH] = dk[src, :].astype(jnp.bfloat16)
                outs[a][rows, (2 + column) * DH : (3 + column) * DH] = dv[src, :].astype(jnp.bfloat16)

    @pl.when(run == 3)
    def _():
        k_gain = gains[0, 1:2, :]
        for j in range(NKB):
            rows = slice(j * KB, (j + 1) * KB)
            c, s = cos_sin(tab[rows, :])
            scaled = dk[rows, :] * SCALE
            dk[rows, :] = scaled
            normed = turn_back(ks[rows, :].astype(jnp.float32), c, s)
            own_k[...] += jnp.sum((turn_back(scaled, c, s) * normed).reshape(KB // 8, 8, DH), 0)

        @pl.when(head == 0)
        def _():
            write(0)

        @pl.when(head == 1)
        def _():
            write(1)
            sums = jnp.concatenate(
                [
                    jnp.sum(own_q[...], 0, keepdims=True),
                    jnp.sum(own_k[...], 0, keepdims=True) / k_gain,
                ],
                0,
            )
            own_out[...] = sums
            for a in range(SHARDS):
                outs[a][TOK:, :] = jnp.zeros((PAD, 4 * DH), jnp.bfloat16)


def attention(blk, side, query, q_far, out_grad, g_far, tab, gains, shards):
    width = GROUP * DH
    near = pl.BlockSpec((1, RUN, width), lambda g, r, b, s: (0, jnp.minimum(r, 1), s[0] * 2 + g))
    far = pl.BlockSpec((RUN, width), lambda g, r, b, s: (jnp.maximum(r - 2, 0), g))
    own = pl.BlockSpec((RUN, width), lambda g, r, b, s: (jnp.minimum(r, 1), g))
    block = pl.BlockSpec((TOK + PAD, 4 * DH), lambda g, r, b, s: (0, 0))
    half = jax.ShapeDtypeStruct((TOK, HALF), jnp.bfloat16)
    shard = jax.ShapeDtypeStruct((TOK + PAD, 4 * DH), jnp.bfloat16)
    low, full = jnp.bfloat16, jnp.float32
    result = pl.pallas_call(
        attention_kernel,
        out_shape=(half, half, half, half) + (shard,) * SHARDS + (jax.ShapeDtypeStruct((2, DH), full),),
        grid_spec=pltpu.PrefetchScalarGridSpec(
            num_scalar_prefetch=2,
            grid=(2, 4),
            in_specs=[
                near,
                far,
                near,
                far,
                pl.BlockSpec((SEQ, DH), lambda g, r, b, s: (0, 0)),
                pl.BlockSpec((1, 2, DH), lambda g, r, b, s: (0, 0, 0)),
            ]
            + [block] * SHARDS,
            out_specs=(own, far, own, far) + (block,) * SHARDS + (pl.BlockSpec((2, DH), lambda g, r, b, s: (0, 0)),),
            scratch_shapes=[
                pltpu.VMEM((SEQ, DH), low),
                pltpu.VMEM((SEQ, DH), low),
                pltpu.VMEM((NKB, DH, KB), low),
                pltpu.VMEM((NKB, DH, KB), low),
                pltpu.VMEM((SEQ, QROWS), full),
                pltpu.VMEM((SEQ, QROWS), low),
                pltpu.VMEM((SEQ, DH), full),
                pltpu.VMEM((SEQ, DH), full),
                pltpu.VMEM((DH, QROWS), full),
                pltpu.VMEM((DH, QROWS), full),
                pltpu.VMEM((8, DH), full),
                pltpu.VMEM((8, DH), full),
            ],
        ),
        compiler_params=pltpu.CompilerParams(vmem_limit_bytes=48 * 1024 * 1024),
        name="attention",
    )(blk, side, query, q_far, out_grad, g_far, tab, gains, *shards)
    return result[:4], result[4 : 4 + SHARDS], result[4 + SHARDS]


def finish_kernel(pos, side, key, tab, gains, near, far, key_grad, value_grad):
    cosine, sine = cos_sin(tab[...])
    gain = gains[0, 1:2, :]
    upper = side[0] == 1
    a = near[...]
    b = far[...].astype(jnp.float32)
    first = jnp.where(upper, b, a)
    second = jnp.where(upper, a, b)
    both = (first, second)
    for head in range(HK):
        half, place = both[head // 2], head % 2
        lanes = slice(head * DH, (head + 1) * DH)
        x = key[0, :, lanes].astype(jnp.float32)
        inverse = lax.rsqrt(jnp.mean(x * x, -1, keepdims=True) + EPS)
        normed = x * inverse
        scaled = turn_back(half[:, place * DH : (place + 1) * DH], cosine, sine)
        grad_normed = scaled * gain
        inner = jnp.mean(grad_normed * normed, -1, keepdims=True)
        key_grad[0, :, lanes] = (inverse * (grad_normed - normed * inner)).astype(jnp.bfloat16)
        value_grad[0, :, lanes] = half[:, (2 + place) * DH : (3 + place) * DH].astype(jnp.bfloat16)


def finish(positions, side, key, tab, gains, near, far):
    out = jax.ShapeDtypeStruct((1, TOK, HK * DH), jnp.bfloat16)
    rows = pl.BlockSpec((1, RUN, HK * DH), lambda r, p, s: (0, r, 0))
    block = pl.BlockSpec((RUN, 4 * DH), lambda r, p, s: (r, 0))
    return pl.pallas_call(
        finish_kernel,
        out_shape=(out, out),
        grid_spec=pltpu.PrefetchScalarGridSpec(
            num_scalar_prefetch=2,
            grid=(2,),
            in_specs=[
                rows,
                pl.BlockSpec((RUN, DH), lambda r, p, s: (p[0, r * RUN] // RUN, 0)),
                pl.BlockSpec((1, 2, DH), lambda r, p, s: (0, 0, 0)),
                block,
                block,
            ],
            out_specs=(rows, rows),
        ),
        name="finish",
    )(positions, side, key, tab, gains, near, far)


def along_z(x, by, depth):
    pairs = [(s * depth + z, s * depth + (z + by) % depth) for s in range(2) for z in range(depth)]
    return lax.ppermute(x, "ctx", pairs)


def across(x, depth):
    return lax.ppermute(x, "ctx", [(i, (i + depth) % (2 * depth)) for i in range(2 * depth)])


def body(query, key, value, out_grad, positions, gains):
    count = lax.axis_size("ctx")
    depth = count // 2
    pipes = lax.axis_size("pipe")
    upper = lax.axis_index("ctx") // depth
    side = upper.astype(jnp.int32).reshape(1)
    tab = jnp.asarray(rope_table())
    mine, other = prep(positions, side, key, value, tab, gains)

    got = across(other, depth)
    start = (1 - upper) * HALF
    q_far = across(lax.dynamic_slice(query[0], (0, start), (TOK, HALF)), depth)
    g_far = across(lax.dynamic_slice(out_grad[0], (0, start), (TOK, HALF)), depth)

    def gather(block):
        ups, downs = [], []
        up = down = block
        for step in range(4):
            up = along_z(up, 1, depth)
            ups.append(up)
            if step < 3:
                down = along_z(down, -1, depth)
                downs.append(down)
        return ups, downs

    ups_a, downs_a = gather(mine)
    ups_b, downs_b = gather(got)
    pairs = [(mine, got)] + list(zip(ups_a, ups_b)) + list(zip(downs_a, downs_b))
    shards = [s for pair in pairs for s in pair]
    blk = jnp.stack([s[TOK, :2] for s in shards]).reshape(2 * SHARDS).astype(jnp.int32)

    halves, grads, own = attention(blk, side, query, q_far, out_grad, g_far, tab, gains, shards)
    att_own, att_far, dq_own, dq_far = halves
    att_got = across(att_far, depth)
    dq_got = across(dq_far, depth)

    high = own.astype(jnp.bfloat16)
    rest = (own - high.astype(jnp.float32)).astype(jnp.bfloat16)
    terms = jnp.concatenate([high, rest], 0)

    def scatter(column):
        part = [grads[2 * i + column] for i in range(8)]
        ups, downs = part[1:5], part[5:8]
        carry_terms = column == 1
        down, up = ups[3], downs[2]
        if carry_terms:
            down = lax.dynamic_update_slice(down, terms, (TOK, 0))
            up = lax.dynamic_update_slice(up, terms, (TOK, 0))
        heard = []
        total = part[0][:TOK].astype(jnp.float32)
        for step in range(4):
            down = along_z(down, -1, depth)
            heard.append(down[TOK : TOK + 4, :DH])
            if step < 3:
                down = (down.astype(jnp.float32) + ups[2 - step].astype(jnp.float32)).astype(jnp.bfloat16)
                up = along_z(up, 1, depth)
                heard.append(up[TOK : TOK + 4, :DH])
                if step < 2:
                    up = (up.astype(jnp.float32) + downs[1 - step].astype(jnp.float32)).astype(jnp.bfloat16)
        total = total + down[:TOK].astype(jnp.float32) + up[:TOK].astype(jnp.float32)
        return total, heard

    far_total, heard = scatter(1)
    near_total, _ = scatter(0)
    gain_sum = own
    for h in heard:
        gain_sum = gain_sum + h[:2].astype(jnp.float32) + h[2:].astype(jnp.float32)

    back = across(far_total.astype(jnp.bfloat16), depth)
    gain_sum = gain_sum + across(gain_sum, depth)
    mirrored = lax.ppermute(gain_sum, "pipe", [(i, pipes - 1 - i) for i in range(pipes)])
    gain_grad = gain_sum + mirrored

    key_grad, value_grad = finish(positions, side, key, tab, gains, near_total, back)

    def joined(near, far):
        lower = jnp.concatenate([near, far], 1)
        higher = jnp.concatenate([far, near], 1)
        return jnp.where(upper == 0, lower, higher)[None]

    return (
        joined(att_own, att_got),
        joined(dq_own, dq_got),
        key_grad,
        value_grad,
        gain_grad[None],
    )


def solution(mesh):
    seq = P("pipe", "ctx", None)
    in_specs = (seq, seq, seq, seq, P("pipe", "ctx"), P("pipe", None, None))
    out_specs = (seq, seq, seq, seq, P("pipe", None, None))
    return jax.shard_map(body, mesh=mesh, in_specs=in_specs, out_specs=out_specs, check_vma=False)
```

time: 829 us -> 161 us (0.19)
  waiting for transfers between devices: 208 us -> 36 us
  matrix products: 128 us -> 0 us
  starting transfers between devices: 172 us -> 48.9 us
  other arithmetic: 116 us -> 7.6 us
  local copies, waits for them, and re-layouts: 103 us -> 12.6 us
  blocking collectives: 67.8 us -> 0 us
  Pallas kernels: 0 us -> 52.7 us
  between operations: 15.1 us -> 0.95 us
  loops' own time: 11 us -> 0 us
    dot_general x57 -> x0, matrix products: 128 us -> none  [the longest x11 38.3 us: grad_tile(): jnp.einsum('qgrk,kgd->qgrd', d_score, k_head, preferred_element_type=jnp....]
    ppermute x68 -> x36, starting transfers between devices: 172 us -> 48.9 us  [the longest x28 39.4 us: along_z(): return lax.ppermute(x, 'ctx', pairs)]
    all_gather x2 -> x0, waiting for transfers between devices: 93.4 us -> none  [the longest x1 71.5 us: body(): v_piece = lax.all_gather(values, 'ctx', axis=0, tiled=True)]
    ppermute x68 -> x36, waiting for transfers between devices: 114 us -> 36 us  [the longest x28 25 us: along_z(): return lax.ppermute(x, 'ctx', pairs)]
    pallas_call x0 -> x3, Pallas kernels: none -> 52.7 us  [the longest x1 46.8 us: attention(): pl.pallas_call(attention_kernel, out_shape=(half, half, half, half) + (sh...]
    psum x1 -> x0, blocking collectives: 38.1 us -> none  [body(): summed = lax.psum(own, 'ctx')]
    reshape x25 -> x0, local copies, waits for them, and re-layouts: 36.9 us -> none  [the longest x11 17.4 us: grad_tile(): v_head = v_block.reshape(width, HK, DH)]
    all_gather x1 -> x0, blocking collectives: 29.7 us -> none  [body(): every_pos = lax.all_gather(positions, 'ctx', axis=1, tiled=True)[0]]
  transfers between devices with their start and end apart: 70 -> 36, of which waited for: 55 -> 13; matrix products, arithmetic and copies ran while one was open for 2% -> 7% of each run, Pallas kernels for 0% -> 0%
where the time goes in v1:
time: 161 us; the launch traced here: 159 us
  Pallas kernels  52.7 us (33%)
  starting transfers between devices  48.9 us (30%)
  waiting for transfers between devices  36 us (22%)
  local copies, waits for them, and re-layouts  12.6 us (8%)
  other arithmetic  7.6 us (5%)
    pallas_call x1, Pallas kernels, attention(): pl.pallas_call(attention_kernel, out_shape=(half, half, half, half) + (sh...  46.8 us
    ppermute x28, starting transfers between devices, along_z(): return lax.ppermute(x, 'ctx', pairs)  39.4 us
    ppermute x28, waiting for transfers between devices, along_z(): return lax.ppermute(x, 'ctx', pairs)  25 us
    ppermute x7, starting transfers between devices, across(): lax.ppermute(x, 'ctx', [(i, (i + depth) % (2 * depth)) for i in range(2 *...  9.53 us
    unnamed x46, local copies, waits for them, and re-layouts  8.87 us
    ppermute x1, waiting for transfers between devices, body(): lax.ppermute(gain_sum, 'pipe', [(i, pipes - 1 - i) for i in range(pipes)])  5.81 us
    ppermute x7, waiting for transfers between devices, across(): lax.ppermute(x, 'ctx', [(i, (i + depth) % (2 * depth)) for i in range(2 *...  5.23 us
  transfers between devices with their start and end apart: 36, of which 13 were waited for; matrix products, arithmetic and copies ran while one was open for 7% of the time, Pallas kernels for 0%

profile of v1, /device:TPU:120, one launch (start us, length us, event | category | flops | bytes accessed | tf_op | source)
XLA Modules:
  0.0 158.8 jit_solution(10757007506963836020)
XLA Ops:
  0.7 2.9 %prep.1 = (bf16[144,512]{1,0:T(8,128)(2,1)}, bf16[144,512]{1,0:T(8,128)(2,1)}) custom-call(s32[1,128]{1,0:T(1,128)} %pos.3, s32[1]{0:T(128)} %bitcast.side, bf16[1,128,512]{2,1,0:T(8,128)(2,1)} %key.3, bf16[1,128,512]{2,1,0:T(8,128)(2,1)} %value.1, f32[2048,128]{1,0:T(8,128)} %constant.32.clone.tab.refs_4_, f32[1,2,128]{2,1,0:T(2,128)} %gains.3), custom_call_target="tpu_custom_call" | custom-call | tf_op jit(solution)/shard_map/prep/pallas_call | solution.py:90
  3.6 3.1 %collective-permute-start.1 = (bf16[144,512]{1,0:T(8,128)(2,1)}, bf16[144,512]{1,0:T(8,128)(2,1)S(1)}, u32[]{:S(2)}, u32[]{:S(2)}) collective-permute-start(bf16[144,512]{1,0:T(8,128)(2,1)} %get-tuple-element.30.refs_6_), channel_id=1, source_target_pairs={{0,1},{1,2},{2,3},{3,4},{4,5},{5,6},{6,7},{7,0},{8,9},{9,10},{10,1... | collective-permute-start | bytes 442376 | tf_op jit(solution)/shard_map/ppermute | solution.py:361
  6.7 1.5 collective-permute-start
  8.2 0.8 dynamic-slice_bitcast_fusion.1
  9.6 3.8 %collective-permute-done.refs_7_ = bf16[144,512]{1,0:T(8,128)(2,1)S(1)} collective-permute-done((bf16[144,512]{1,0:T(8,128)(2,1)}, bf16[144,512]{1,0:T(8,128)(2,1)S(1)}, u32[]{:S(2)}, u32[]{:S(2)}) %collective-permute-start) | collective-permute-done | bytes 147488 | tf_op jit(solution)/shard_map/ppermute | solution.py:365
  13.4 3.2 %collective-permute-start.2 = (bf16[144,512]{1,0:T(8,128)(2,1)S(1)}, bf16[144,512]{1,0:T(8,128)(2,1)S(1)}, u32[]{:S(2)}, u32[]{:S(2)}) collective-permute-start(bf16[144,512]{1,0:T(8,128)(2,1)S(1)} %collective-permute-done.refs_7_), channel_id=1, source_target_pairs={{0,1},{1,2},{2,3},{3,4},{4,5},{5,6},{6,7},{7,0},{8,9},{9,10},{10,1... | collective-permute-start | bytes 442376 | tf_op jit(solution)/shard_map/ppermute | solution.py:361
  16.6 3.2 %collective-permute-start.3 = (bf16[144,512]{1,0:T(8,128)(2,1)S(1)}, bf16[144,512]{1,0:T(8,128)(2,1)S(1)}, u32[]{:S(2)}, u32[]{:S(2)}) collective-permute-start(bf16[144,512]{1,0:T(8,128)(2,1)S(1)} %collective-permute-done.1.refs_8_), channel_id=1, source_target_pairs={{0,1},{1,2},{2,3},{3,4},{4,5},{5,6},{6,7},{7,0},{8,9},{9,10},{10,1... | collective-permute-start | bytes 442376 | tf_op jit(solution)/shard_map/ppermute | solution.py:361
  19.8 0.8 dynamic-slice_bitcast_fusion
  20.7 1.8 %collective-permute-start.16 = (bf16[128,2048]{1,0:T(8,128)(2,1)}, bf16[128,2048]{1,0:T(8,128)(2,1)}, u32[]{:S(2)}, u32[]{:S(2)}) collective-permute-start(bf16[128,2048]{1,0:T(8,128)(2,1)} %dynamic-slice_bitcast_fusion), channel_id=1, source_target_pairs={{0,8},{1,9},{2,10},{3,11},{4,12},{5,13},{6,14},{7,15},{8,0},{9,1},... | collective-permute-start | bytes 1572872 | tf_op jit(solution)/shard_map/ppermute | solution.py:365
  22.5 3.7 %collective-permute-start.4 = (bf16[144,512]{1,0:T(8,128)(2,1)S(1)}, bf16[144,512]{1,0:T(8,128)(2,1)S(1)}, u32[]{:S(2)}, u32[]{:S(2)}) collective-permute-start(bf16[144,512]{1,0:T(8,128)(2,1)S(1)} %collective-permute-done.2.refs_9_), channel_id=1, source_target_pairs={{0,1},{1,2},{2,3},{3,4},{4,5},{5,6},{6,7},{7,0},{8,9},{9,10},{10,1... | collective-permute-start | bytes 442376 | tf_op jit(solution)/shard_map/ppermute | solution.py:361
  26.3 3.3 %collective-permute-done.11.refs_18_ = bf16[144,512]{1,0:T(8,128)(2,1)S(1)} collective-permute-done((bf16[144,512]{1,0:T(8,128)(2,1)S(1)}, bf16[144,512]{1,0:T(8,128)(2,1)S(1)}, u32[]{:S(2)}, u32[]{:S(2)}) %collective-permute-start.11) | collective-permute-done | bytes 147488 | tf_op jit(solution)/shard_map/ppermute | solution.py:361
  29.6 2.5 %collective-permute-done.5.refs_12_ = bf16[144,512]{1,0:T(8,128)(2,1)S(1)} collective-permute-done((bf16[144,512]{1,0:T(8,128)(2,1)S(1)}, bf16[144,512]{1,0:T(8,128)(2,1)S(1)}, u32[]{:S(2)}, u32[]{:S(2)}) %collective-permute-start.5) | collective-permute-done | bytes 147488 | tf_op jit(solution)/shard_map/ppermute | solution.py:361
  32.1 3.2 %collective-permute-start.6 = (bf16[144,512]{1,0:T(8,128)(2,1)S(1)}, bf16[144,512]{1,0:T(8,128)(2,1)S(1)}, u32[]{:S(2)}, u32[]{:S(2)}) collective-permute-start(bf16[144,512]{1,0:T(8,128)(2,1)S(1)} %collective-permute-done.4.refs_11_), channel_id=1, source_target_pairs={{0,1},{1,2},{2,3},{3,4},{4,5},{5,6},{6,7},{7,0},{8,9},{9,10},{10,1... | collective-permute-start | bytes 442376 | tf_op jit(solution)/shard_map/ppermute | solution.py:361
  35.4 0.8 collective-permute-done.12.refs_19_
  36.2 2.9 %collective-permute-done.13.refs_20_ = bf16[144,512]{1,0:T(8,128)(2,1)S(1)} collective-permute-done((bf16[144,512]{1,0:T(8,128)(2,1)S(1)}, bf16[144,512]{1,0:T(8,128)(2,1)S(1)}, u32[]{:S(2)}, u32[]{:S(2)}) %collective-permute-start.13) | collective-permute-done | bytes 147488 | tf_op jit(solution)/shard_map/ppermute | solution.py:361
  39.1 3.5 %collective-permute-start.8 = (bf16[144,512]{1,0:T(8,128)(2,1)S(1)}, bf16[144,512]{1,0:T(8,128)(2,1)S(1)}, u32[]{:S(2)}, u32[]{:S(2)}) collective-permute-start(bf16[144,512]{1,0:T(8,128)(2,1)S(1)} %collective-permute-done.6.refs_13_), channel_id=1, source_target_pairs={{0,1},{1,2},{2,3},{3,4},{4,5},{5,6},{6,7},{7,0},{8,9},{9,10},{10,1... | collective-permute-start | bytes 442376 | tf_op jit(solution)/shard_map/ppermute | solution.py:361
  44.2 1.3 collective-permute-done.14.refs_21_
  46.0 0.8 copy-done.20
  46.8 46.8 %attention.1 = (bf16[128,2048]{1,0:T(8,128)(2,1)S(1)}, bf16[128,2048]{1,0:T(8,128)(2,1)S(1)}, bf16[128,2048]{1,0:T(8,128)(2,1)}, bf16[128,2048]{1,0:T(8,128)(2,1...) custom-call(s32[32]{0:T(128)S(1)} %reshape.129.blk, ...), custom_call_target="tpu_custom_call" | custom-call | tf_op jit(solution)/shard_map/attention/pallas_call | solution.py:277
  93.6 0.7 copy-done.1
  94.9 0.7 copy-done.5
  96.3 0.7 copy-done.8
  96.9 0.7 copy-done.9
  97.6 0.7 copy-done.10
  98.9 0.8 copy-done.15
  101.6 6.8 %collective-permute-start.30 = (bf16[144,512]{1,0:T(8,128)(2,1)}, bf16[144,512]{1,0:T(8,128)(2,1)S(1)}, u32[]{:S(2)}, u32[]{:S(2)}) collective-permute-start(bf16[144,512]{1,0:T(8,128)(2,1)} %get-tuple-element.56), channel_id=1, source_target_pairs={{0,1},{1,2},{2,3},{3,4},{4,5},{5,6},{6,7},{7,0},{8,9},{9,10},{10,1... | collective-permute-start | bytes 442376 | tf_op jit(solution)/shard_map/ppermute | solution.py:361
  108.4 3.2 %collective-permute-start.23 = (bf16[144,512]{1,0:T(8,128)(2,1)}, bf16[144,512]{1,0:T(8,128)(2,1)S(1)}, u32[]{:S(2)}, u32[]{:S(2)}) collective-permute-start(bf16[144,512]{1,0:T(8,128)(2,1)} %copy-done.16), channel_id=1, source_target_pairs={{0,1},{1,2},{2,3},{3,4},{4,5},{5,6},{6,7},{7,0},{8,9},{9,10},{10,1... | collective-permute-start | bytes 442376 | tf_op jit(solution)/shard_map/ppermute | solution.py:361
  111.6 3.4 %collective-permute-start.18 = (bf16[128,2048]{1,0:T(8,128)(2,1)}, bf16[128,2048]{1,0:T(8,128)(2,1)S(1)}, u32[]{:S(2)}, u32[]{:S(2)}) collective-permute-start(bf16[128,2048]{1,0:T(8,128)(2,1)} %get-tuple-element.35), channel_id=1, source_target_pairs={{0,8},{1,9},{2,10},{3,11},{4,12},{5,13},{6,14},{7,15},{8,0},{9,1},... | collective-permute-start | bytes 1572872 | tf_op jit(solution)/shard_map/ppermute | solution.py:365
  115.1 1.0 add_convert_fusion.4
  116.2 0.9 add_convert_fusion.1
  117.2 3.3 %collective-permute-start.31 = (bf16[144,512]{1,0:T(8,128)(2,1)S(1)}, bf16[144,512]{1,0:T(8,128)(2,1)S(1)}, u32[]{:S(2)}, u32[]{:S(2)}) collective-permute-start(bf16[144,512]{1,0:T(8,128)(2,1)S(1)} %add_convert_fusion.1), channel_id=1, source_target_pairs={{0,1},{1,2},{2,3},{3,4},{4,5},{5,6},{6,7},{7,0},{8,9},{9,10},{10,1... | collective-permute-start | bytes 442376 | tf_op jit(solution)/shard_map/ppermute | solution.py:361
  120.5 0.9 add_convert_fusion.9
  121.6 1.7 %collective-permute-done.27 = bf16[144,512]{1,0:T(8,128)(2,1)S(1)} collective-permute-done((bf16[144,512]{1,0:T(8,128)(2,1)S(1)}, bf16[144,512]{1,0:T(8,128)(2,1)S(1)}, u32[]{:S(2)}, u32[]{:S(2)}) %collective-permute-start.27) | collective-permute-done | bytes 147488 | tf_op jit(solution)/shard_map/ppermute | solution.py:361
  123.2 2.3 %collective-permute-start.24 = (bf16[144,512]{1,0:T(8,128)(2,1)S(1)}, bf16[144,512]{1,0:T(8,128)(2,1)S(1)}, u32[]{:S(2)}, u32[]{:S(2)}) collective-permute-start(bf16[144,512]{1,0:T(8,128)(2,1)S(1)} %add_convert_fusion.6), channel_id=1, source_target_pairs={{0,1},{1,2},{2,3},{3,4},{4,5},{5,6},{6,7},{7,0},{8,9},{9,10},{10,1... | collective-permute-start | bytes 442376 | tf_op jit(solution)/shard_map/ppermute | solution.py:361
  125.9 3.4 %collective-permute-done.20 = bf16[144,512]{1,0:T(8,128)(2,1)S(1)} collective-permute-done((bf16[144,512]{1,0:T(8,128)(2,1)S(1)}, bf16[144,512]{1,0:T(8,128)(2,1)S(1)}, u32[]{:S(2)}, u32[]{:S(2)}) %collective-permute-start.20) | collective-permute-done | bytes 147488 | tf_op jit(solution)/shard_map/ppermute | solution.py:361
  129.9 1.6 %collective-permute-start.21 = (bf16[144,512]{1,0:T(8,128)(2,1)S(1)}, bf16[144,512]{1,0:T(8,128)(2,1)S(1)}, u32[]{:S(2)}, u32[]{:S(2)}) collective-permute-start(bf16[144,512]{1,0:T(8,128)(2,1)S(1)} %add_convert_fusion.8), channel_id=1, source_target_pairs={{0,7},{1,0},{2,1},{3,2},{4,3},{5,4},{6,5},{7,6},{8,15},{9,8},{10,9... | collective-permute-start | bytes 442376 | tf_op jit(solution)/shard_map/ppermute | solution.py:361
  131.5 0.7 collective-permute-done.28
  132.2 1.1 collective-permute-start.25
  133.3 4.6 %collective-permute-done.21 = bf16[144,512]{1,0:T(8,128)(2,1)S(1)} collective-permute-done((bf16[144,512]{1,0:T(8,128)(2,1)S(1)}, bf16[144,512]{1,0:T(8,128)(2,1)S(1)}, u32[]{:S(2)}, u32[]{:S(2)}) %collective-permute-start.21) | collective-permute-done | bytes 147488 | tf_op jit(solution)/shard_map/ppermute | solution.py:361
  138.1 1.2 maximum_select_fusion.1
  139.3 1.2 maximum_select_fusion
  140.5 3.8 %collective-permute-done.29 = bf16[144,512]{1,0:T(8,128)(2,1)S(1)} collective-permute-done((bf16[144,512]{1,0:T(8,128)(2,1)S(1)}, bf16[144,512]{1,0:T(8,128)(2,1)S(1)}, u32[]{:S(2)}, u32[]{:S(2)}) %collective-permute-start.29) | collective-permute-done | bytes 147488 | tf_op jit(solution)/shard_map/ppermute | solution.py:361
  144.3 1.5 collective-permute-start.34
  145.9 0.7 collective-permute-start.33
  146.6 1.4 collective-permute-done.34
  148.0 0.8 convert_add_fusion.near
  148.7 5.8 %collective-permute-done.35 = f32[2,128]{1,0:T(2,128)S(1)} collective-permute-done((f32[2,128]{1,0:T(2,128)S(1)}, f32[2,128]{1,0:T(2,128)S(1)}, u32[]{:S(2)}, u32[]{:S(2)}) %collective-permute-start.35) | collective-permute-done | bytes 1056 | tf_op jit(solution)/shard_map/ppermute | solution.py:438
  155.8 3.0 %finish.1 = (bf16[1,128,512]{2,1,0:T(8,128)(2,1)}, bf16[1,128,512]{2,1,0:T(8,128)(2,1)}) custom-call(s32[1,128]{1,0:T(1,128)} %pos.3, s32[1]{0:T(128)} %bitcast.side, bf16[1,128,512]{2,1,0:T(8,128)(2,1)} %key.3, f32[2048,128]{1,0:T(8,128)} %constant.32.clone.tab.refs_4_, f32[1,2,128]{2,1,0:T(2,128)} %gains.3, f32[128,512]{1,0:T(8,128)} %convert_add_fusion.near, ...), custom_call_target="tpu_custom_call" | custom-call | tf_op jit(solution)/shard_map/finish/pallas_call | solution.py:340
  (130 shorter events, 9.3 us)
Async XLA Ops:
  0.6 7.6 %copy-start.18 = (bf16[1,128,4096]{2,1,0:T(8,128)(2,1)S(1)}, bf16[1,128,4096]{2,1,0:T(8,128)(2,1)}, u32[]{:S(2)}) copy-start(bf16[1,128,4096]{2,1,0:T(8,128)(2,1)} %refs_0_.1) | copy-start | bytes 3145732
  0.7 19.2 %copy-start.19 = (bf16[1,128,4096]{2,1,0:T(8,128)(2,1)S(1)}, bf16[1,128,4096]{2,1,0:T(8,128)(2,1)}, u32[]{:S(2)}) copy-start(bf16[1,128,4096]{2,1,0:T(8,128)(2,1)} %refs_2_.1) | copy-start | bytes 3145732
  3.6 13.0 %collective-permute-start.1 = (bf16[144,512]{1,0:T(8,128)(2,1)}, bf16[144,512]{1,0:T(8,128)(2,1)S(1)}, u32[]{:S(2)}, u32[]{:S(2)}) collective-permute-start(bf16[144,512]{1,0:T(8,128)(2,1)} %get-tuple-element.30.refs_6_), channel_id=1, source_target_pairs={{0,1},{1,2},{2,3},{3,4},{4,5},{5,6},{6,7},{7,0},{8,9},{9,10},{10,1... | collective-permute-start | bytes 442376 | tf_op jit(solution)/shard_map/ppermute | solution.py:361
  6.7 14.0 %collective-permute-start.9 = (bf16[144,512]{1,0:T(8,128)(2,1)}, bf16[144,512]{1,0:T(8,128)(2,1)S(1)}, u32[]{:S(2)}, u32[]{:S(2)}) collective-permute-start(bf16[144,512]{1,0:T(8,128)(2,1)} %get-tuple-element.30.refs_6_), channel_id=1, source_target_pairs={{0,7},{1,0},{2,1},{3,2},{4,3},{5,4},{6,5},{7,6},{8,15},{9,8},{10,9... | collective-permute-start | bytes 442376 | tf_op jit(solution)/shard_map/ppermute | solution.py:361
  6.7 6.7 %collective-permute-start = (bf16[144,512]{1,0:T(8,128)(2,1)}, bf16[144,512]{1,0:T(8,128)(2,1)S(1)}, u32[]{:S(2)}, u32[]{:S(2)}) collective-permute-start(bf16[144,512]{1,0:T(8,128)(2,1)} %get-tuple-element.31), channel_id=1, source_target_pairs={{0,8},{1,9},{2,10},{3,11},{4,12},{5,13},{6,14},{7,15},{8,0},{9,1},... | collective-permute-start | bytes 442376 | tf_op jit(solution)/shard_map/ppermute | solution.py:365
  8.2 34.4 %copy-start = (bf16[144,512]{1,0:T(8,128)(2,1)S(1)}, bf16[144,512]{1,0:T(8,128)(2,1)}, u32[]{:S(2)}) copy-start(bf16[144,512]{1,0:T(8,128)(2,1)} %get-tuple-element.30.refs_6_) | copy-start | bytes 442372
  8.2 38.6 %copy-start.14 = (f32[1,2,128]{2,1,0:T(2,128)S(1)}, f32[1,2,128]{2,1,0:T(2,128)}, u32[]{:S(2)}) copy-start(f32[1,2,128]{2,1,0:T(2,128)} %gains.3) | copy-start | bytes 3076
  9.0 37.0 %collective-permute-start.15 = (bf16[128,2048]{1,0:T(8,128)(2,1)}, bf16[128,2048]{1,0:T(8,128)(2,1)S(1)}, u32[]{:S(2)}, u32[]{:S(2)}) collective-permute-start(bf16[128,2048]{1,0:T(8,128)(2,1)} %dynamic-slice_bitcast_fusion.1), channel_id=1, source_target_pairs={{0,8},{1,9},{2,10},{3,11},{4,12},{5,13},{6,14},{7,15},{8,0},{9,1},... | collective-permute-start | bytes 1572872 | tf_op jit(solution)/shard_map/ppermute | solution.py:365
  13.4 9.1 %collective-permute-start.2 = (bf16[144,512]{1,0:T(8,128)(2,1)S(1)}, bf16[144,512]{1,0:T(8,128)(2,1)S(1)}, u32[]{:S(2)}, u32[]{:S(2)}) collective-permute-start(bf16[144,512]{1,0:T(8,128)(2,1)S(1)} %collective-permute-done.refs_7_), channel_id=1, source_target_pairs={{0,1},{1,2},{2,3},{3,4},{4,5},{5,6},{6,7},{7,0},{8,9},{9,10},{10,1... | collective-permute-start | bytes 442376 | tf_op jit(solution)/shard_map/ppermute | solution.py:361
  16.6 9.7 %collective-permute-start.10 = (bf16[144,512]{1,0:T(8,128)(2,1)S(1)}, bf16[144,512]{1,0:T(8,128)(2,1)S(1)}, u32[]{:S(2)}, u32[]{:S(2)}) collective-permute-start(bf16[144,512]{1,0:T(8,128)(2,1)S(1)} %collective-permute-done.refs_7_), channel_id=1, source_target_pairs={{0,7},{1,0},{2,1},{3,2},{4,3},{5,4},{6,5},{7,6},{8,15},{9,8},{10,9... | collective-permute-start | bytes 442376 | tf_op jit(solution)/shard_map/ppermute | solution.py:361
  16.6 5.9 %collective-permute-start.3 = (bf16[144,512]{1,0:T(8,128)(2,1)S(1)}, bf16[144,512]{1,0:T(8,128)(2,1)S(1)}, u32[]{:S(2)}, u32[]{:S(2)}) collective-permute-start(bf16[144,512]{1,0:T(8,128)(2,1)S(1)} %collective-permute-done.1.refs_8_), channel_id=1, source_target_pairs={{0,1},{1,2},{2,3},{3,4},{4,5},{5,6},{6,7},{7,0},{8,9},{9,10},{10,1... | collective-permute-start | bytes 442376 | tf_op jit(solution)/shard_map/ppermute | solution.py:361
  20.7 26.1 %collective-permute-start.16 = (bf16[128,2048]{1,0:T(8,128)(2,1)}, bf16[128,2048]{1,0:T(8,128)(2,1)}, u32[]{:S(2)}, u32[]{:S(2)}) collective-permute-start(bf16[128,2048]{1,0:T(8,128)(2,1)} %dynamic-slice_bitcast_fusion), channel_id=1, source_target_pairs={{0,8},{1,9},{2,10},{3,11},{4,12},{5,13},{6,14},{7,15},{8,0},{9,1},... | collective-permute-start | bytes 1572872 | tf_op jit(solution)/shard_map/ppermute | solution.py:365
  22.5 7.1 %collective-permute-start.11 = (bf16[144,512]{1,0:T(8,128)(2,1)S(1)}, bf16[144,512]{1,0:T(8,128)(2,1)S(1)}, u32[]{:S(2)}, u32[]{:S(2)}) collective-permute-start(bf16[144,512]{1,0:T(8,128)(2,1)S(1)} %collective-permute-done.9.refs_16_), channel_id=1, source_target_pairs={{0,7},{1,0},{2,1},{3,2},{4,3},{5,4},{6,5},{7,6},{8,15},{9,8},{10,9... | collective-permute-start | bytes 442376 | tf_op jit(solution)/shard_map/ppermute | solution.py:361
  22.5 7.1 %collective-permute-start.4 = (bf16[144,512]{1,0:T(8,128)(2,1)S(1)}, bf16[144,512]{1,0:T(8,128)(2,1)S(1)}, u32[]{:S(2)}, u32[]{:S(2)}) collective-permute-start(bf16[144,512]{1,0:T(8,128)(2,1)S(1)} %collective-permute-done.2.refs_9_), channel_id=1, source_target_pairs={{0,1},{1,2},{2,3},{3,4},{4,5},{5,6},{6,7},{7,0},{8,9},{9,10},{10,1... | collective-permute-start | bytes 442376 | tf_op jit(solution)/shard_map/ppermute | solution.py:361
  26.3 5.8 %collective-permute-start.5 = (bf16[144,512]{1,0:T(8,128)(2,1)S(1)}, bf16[144,512]{1,0:T(8,128)(2,1)S(1)}, u32[]{:S(2)}, u32[]{:S(2)}) collective-permute-start(bf16[144,512]{1,0:T(8,128)(2,1)S(1)} %collective-permute-done.3.refs_10_), channel_id=1, source_target_pairs={{0,1},{1,2},{2,3},{3,4},{4,5},{5,6},{6,7},{7,0},{8,9},{9,10},{10,1... | collective-permute-start | bytes 442376 | tf_op jit(solution)/shard_map/ppermute | solution.py:361
  29.6 6.6 %collective-permute-start.12 = (bf16[144,512]{1,0:T(8,128)(2,1)S(1)}, bf16[144,512]{1,0:T(8,128)(2,1)S(1)}, u32[]{:S(2)}, u32[]{:S(2)}) collective-permute-start(bf16[144,512]{1,0:T(8,128)(2,1)S(1)} %collective-permute-done.10.refs_17_), channel_id=1, source_target_pairs={{0,7},{1,0},{2,1},{3,2},{4,3},{5,4},{6,5},{7,6},{8,15},{9,8},{10,9... | collective-permute-start | bytes 442376 | tf_op jit(solution)/shard_map/ppermute | solution.py:361
  29.6 9.5 %collective-permute-start.13 = (bf16[144,512]{1,0:T(8,128)(2,1)S(1)}, bf16[144,512]{1,0:T(8,128)(2,1)S(1)}, u32[]{:S(2)}, u32[]{:S(2)}) collective-permute-start(bf16[144,512]{1,0:T(8,128)(2,1)S(1)} %collective-permute-done.11.refs_18_), channel_id=1, source_target_pairs={{0,7},{1,0},{2,1},{3,2},{4,3},{5,4},{6,5},{7,6},{8,15},{9,8},{10,9... | collective-permute-start | bytes 442376 | tf_op jit(solution)/shard_map/ppermute | solution.py:361
  32.1 7.0 %collective-permute-start.6 = (bf16[144,512]{1,0:T(8,128)(2,1)S(1)}, bf16[144,512]{1,0:T(8,128)(2,1)S(1)}, u32[]{:S(2)}, u32[]{:S(2)}) collective-permute-start(bf16[144,512]{1,0:T(8,128)(2,1)S(1)} %collective-permute-done.4.refs_11_), channel_id=1, source_target_pairs={{0,1},{1,2},{2,3},{3,4},{4,5},{5,6},{6,7},{7,0},{8,9},{9,10},{10,1... | collective-permute-start | bytes 442376 | tf_op jit(solution)/shard_map/ppermute | solution.py:361
  36.2 7.7 %collective-permute-start.7 = (bf16[144,512]{1,0:T(8,128)(2,1)S(1)}, bf16[144,512]{1,0:T(8,128)(2,1)S(1)}, u32[]{:S(2)}, u32[]{:S(2)}) collective-permute-start(bf16[144,512]{1,0:T(8,128)(2,1)S(1)} %collective-permute-done.5.refs_12_), channel_id=1, source_target_pairs={{0,1},{1,2},{2,3},{3,4},{4,5},{5,6},{6,7},{7,0},{8,9},{9,10},{10,1... | collective-permute-start | bytes 442376 | tf_op jit(solution)/shard_map/ppermute | solution.py:361
  39.1 6.4 %collective-permute-start.14 = (bf16[144,512]{1,0:T(8,128)(2,1)S(1)}, bf16[144,512]{1,0:T(8,128)(2,1)S(1)}, u32[]{:S(2)}, u32[]{:S(2)}) collective-permute-start(bf16[144,512]{1,0:T(8,128)(2,1)S(1)} %collective-permute-done.12.refs_19_), channel_id=1, source_target_pairs={{0,7},{1,0},{2,1},{3,2},{4,3},{5,4},{6,5},{7,6},{8,15},{9,8},{10,9... | collective-permute-start | bytes 442376 | tf_op jit(solution)/shard_map/ppermute | solution.py:361
  39.1 6.5 %collective-permute-start.8 = (bf16[144,512]{1,0:T(8,128)(2,1)S(1)}, bf16[144,512]{1,0:T(8,128)(2,1)S(1)}, u32[]{:S(2)}, u32[]{:S(2)}) collective-permute-start(bf16[144,512]{1,0:T(8,128)(2,1)S(1)} %collective-permute-done.6.refs_13_), channel_id=1, source_target_pairs={{0,1},{1,2},{2,3},{3,4},{4,5},{5,6},{6,7},{7,0},{8,9},{9,10},{10,1... | collective-permute-start | bytes 442376 | tf_op jit(solution)/shard_map/ppermute | solution.py:361
  46.0 0.8 copy-start.20
  98.9 0.8 copy-start.15
  101.0 20.5 %copy-start.6 = (bf16[144,512]{1,0:T(8,128)(2,1)S(1)}, bf16[144,512]{1,0:T(8,128)(2,1)}, u32[]{:S(2)}) copy-start(bf16[144,512]{1,0:T(8,128)(2,1)} %copy-done.5) | copy-start | bytes 442372
  101.0 24.5 %copy-start.4 = (bf16[144,512]{1,0:T(8,128)(2,1)S(1)}, bf16[144,512]{1,0:T(8,128)(2,1)}, u32[]{:S(2)}) copy-start(bf16[144,512]{1,0:T(8,128)(2,1)} %copy-done.3) | copy-start | bytes 442372
  101.6 13.4 %collective-permute-start.26 = (bf16[144,512]{1,0:T(8,128)(2,1)}, bf16[144,512]{1,0:T(8,128)(2,1)S(1)}, u32[]{:S(2)}, u32[]{:S(2)}) collective-permute-start(bf16[144,512]{1,0:T(8,128)(2,1)} %get-tuple-element.55), channel_id=1, source_target_pairs={{0,7},{1,0},{2,1},{3,2},{4,3},{5,4},{6,5},{7,6},{8,15},{9,8},{10,9... | collective-permute-start | bytes 442376 | tf_op jit(solution)/shard_map/ppermute | solution.py:361
  101.6 14.5 %collective-permute-start.30 = (bf16[144,512]{1,0:T(8,128)(2,1)}, bf16[144,512]{1,0:T(8,128)(2,1)S(1)}, u32[]{:S(2)}, u32[]{:S(2)}) collective-permute-start(bf16[144,512]{1,0:T(8,128)(2,1)} %get-tuple-element.56), channel_id=1, source_target_pairs={{0,1},{1,2},{2,3},{3,4},{4,5},{5,6},{6,7},{7,0},{8,9},{9,10},{10,1... | collective-permute-start | bytes 442376 | tf_op jit(solution)/shard_map/ppermute | solution.py:361
  108.4 8.8 %collective-permute-start.19 = (bf16[144,512]{1,0:T(8,128)(2,1)}, bf16[144,512]{1,0:T(8,128)(2,1)S(1)}, u32[]{:S(2)}, u32[]{:S(2)}) collective-permute-start(bf16[144,512]{1,0:T(8,128)(2,1)} %copy-done.17), channel_id=1, source_target_pairs={{0,7},{1,0},{2,1},{3,2},{4,3},{5,4},{6,5},{7,6},{8,15},{9,8},{10,9... | collective-permute-start | bytes 442376 | tf_op jit(solution)/shard_map/ppermute | solution.py:361
  108.4 13.0 %collective-permute-start.23 = (bf16[144,512]{1,0:T(8,128)(2,1)}, bf16[144,512]{1,0:T(8,128)(2,1)S(1)}, u32[]{:S(2)}, u32[]{:S(2)}) collective-permute-start(bf16[144,512]{1,0:T(8,128)(2,1)} %copy-done.16), channel_id=1, source_target_pairs={{0,1},{1,2},{2,3},{3,4},{4,5},{5,6},{6,7},{7,0},{8,9},{9,10},{10,1... | collective-permute-start | bytes 442376 | tf_op jit(solution)/shard_map/ppermute | solution.py:361
  111.6 26.3 %collective-permute-start.18 = (bf16[128,2048]{1,0:T(8,128)(2,1)}, bf16[128,2048]{1,0:T(8,128)(2,1)S(1)}, u32[]{:S(2)}, u32[]{:S(2)}) collective-permute-start(bf16[128,2048]{1,0:T(8,128)(2,1)} %get-tuple-element.35), channel_id=1, source_target_pairs={{0,8},{1,9},{2,10},{3,11},{4,12},{5,13},{6,14},{7,15},{8,0},{9,1},... | collective-permute-start | bytes 1572872 | tf_op jit(solution)/shard_map/ppermute | solution.py:365
  115.0 24.3 %collective-permute-start.17 = (bf16[128,2048]{1,0:T(8,128)(2,1)}, bf16[128,2048]{1,0:T(8,128)(2,1)S(1)}, u32[]{:S(2)}, u32[]{:S(2)}) collective-permute-start(bf16[128,2048]{1,0:T(8,128)(2,1)} %copy-done.15), channel_id=1, source_target_pairs={{0,8},{1,9},{2,10},{3,11},{4,12},{5,13},{6,14},{7,15},{8,0},{9,1},... | collective-permute-start | bytes 1572872 | tf_op jit(solution)/shard_map/ppermute | solution.py:365
  115.1 10.8 %copy-start.2 = (bf16[144,512]{1,0:T(8,128)(2,1)S(1)}, bf16[144,512]{1,0:T(8,128)(2,1)}, u32[]{:S(2)}) copy-start(bf16[144,512]{1,0:T(8,128)(2,1)} %copy-done.1) | copy-start | bytes 442372
  116.1 7.1 %collective-permute-start.27 = (bf16[144,512]{1,0:T(8,128)(2,1)S(1)}, bf16[144,512]{1,0:T(8,128)(2,1)S(1)}, u32[]{:S(2)}, u32[]{:S(2)}) collective-permute-start(bf16[144,512]{1,0:T(8,128)(2,1)S(1)} %add_convert_fusion.4), channel_id=1, source_target_pairs={{0,7},{1,0},{2,1},{3,2},{4,3},{5,4},{6,5},{7,6},{8,15},{9,8},{10,9... | collective-permute-start | bytes 442376 | tf_op jit(solution)/shard_map/ppermute | solution.py:361
  117.2 8.4 %collective-permute-start.31 = (bf16[144,512]{1,0:T(8,128)(2,1)S(1)}, bf16[144,512]{1,0:T(8,128)(2,1)S(1)}, u32[]{:S(2)}, u32[]{:S(2)}) collective-permute-start(bf16[144,512]{1,0:T(8,128)(2,1)S(1)} %add_convert_fusion.1), channel_id=1, source_target_pairs={{0,1},{1,2},{2,3},{3,4},{4,5},{5,6},{6,7},{7,0},{8,9},{9,10},{10,1... | collective-permute-start | bytes 442376 | tf_op jit(solution)/shard_map/ppermute | solution.py:361
  121.4 7.9 %collective-permute-start.20 = (bf16[144,512]{1,0:T(8,128)(2,1)S(1)}, bf16[144,512]{1,0:T(8,128)(2,1)S(1)}, u32[]{:S(2)}, u32[]{:S(2)}) collective-permute-start(bf16[144,512]{1,0:T(8,128)(2,1)S(1)} %add_convert_fusion.9), channel_id=1, source_target_pairs={{0,7},{1,0},{2,1},{3,2},{4,3},{5,4},{6,5},{7,6},{8,15},{9,8},{10,9... | collective-permute-start | bytes 442376 | tf_op jit(solution)/shard_map/ppermute | solution.py:361
  123.2 6.6 %collective-permute-start.24 = (bf16[144,512]{1,0:T(8,128)(2,1)S(1)}, bf16[144,512]{1,0:T(8,128)(2,1)S(1)}, u32[]{:S(2)}, u32[]{:S(2)}) collective-permute-start(bf16[144,512]{1,0:T(8,128)(2,1)S(1)} %add_convert_fusion.6), channel_id=1, source_target_pairs={{0,1},{1,2},{2,3},{3,4},{4,5},{5,6},{6,7},{7,0},{8,9},{9,10},{10,1... | collective-permute-start | bytes 442376 | tf_op jit(solution)/shard_map/ppermute | solution.py:361
  125.6 6.7 %collective-permute-start.28 = (bf16[144,512]{1,0:T(8,128)(2,1)S(1)}, bf16[144,512]{1,0:T(8,128)(2,1)S(1)}, u32[]{:S(2)}, u32[]{:S(2)}) collective-permute-start(bf16[144,512]{1,0:T(8,128)(2,1)S(1)} %add_convert_fusion.3), channel_id=1, source_target_pairs={{0,7},{1,0},{2,1},{3,2},{4,3},{5,4},{6,5},{7,6},{8,15},{9,8},{10,9... | collective-permute-start | bytes 442376 | tf_op jit(solution)/shard_map/ppermute | solution.py:361
  125.9 12.2 %copy-start.21 = (bf16[128,2048]{1,0:T(8,128)(2,1)S(1)}, bf16[128,2048]{1,0:T(8,128)(2,1)}, u32[]{:S(2)}) copy-start(bf16[128,2048]{1,0:T(8,128)(2,1)} %get-tuple-element.34) | copy-start | bytes 1572868
  129.3 11.2 %collective-permute-start.32 = (bf16[144,512]{1,0:T(8,128)(2,1)S(1)}, bf16[144,512]{1,0:T(8,128)(2,1)S(1)}, u32[]{:S(2)}, u32[]{:S(2)}) collective-permute-start(bf16[144,512]{1,0:T(8,128)(2,1)S(1)} %add_convert_fusion), channel_id=1, source_target_pairs={{0,1},{1,2},{2,3},{3,4},{4,5},{5,6},{6,7},{7,0},{8,9},{9,10},{10,1... | collective-permute-start | bytes 442376 | tf_op jit(solution)/shard_map/ppermute | solution.py:361
  129.9 8.1 %collective-permute-start.21 = (bf16[144,512]{1,0:T(8,128)(2,1)S(1)}, bf16[144,512]{1,0:T(8,128)(2,1)S(1)}, u32[]{:S(2)}, u32[]{:S(2)}) collective-permute-start(bf16[144,512]{1,0:T(8,128)(2,1)S(1)} %add_convert_fusion.8), channel_id=1, source_target_pairs={{0,7},{1,0},{2,1},{3,2},{4,3},{5,4},{6,5},{7,6},{8,15},{9,8},{10,9... | collective-permute-start | bytes 442376 | tf_op jit(solution)/shard_map/ppermute | solution.py:361
  132.2 15.7 %collective-permute-start.25 = (bf16[144,512]{1,0:T(8,128)(2,1)S(1)}, bf16[144,512]{1,0:T(8,128)(2,1)S(1)}, u32[]{:S(2)}, u32[]{:S(2)}) collective-permute-start(bf16[144,512]{1,0:T(8,128)(2,1)S(1)} %add_convert_fusion.5), channel_id=1, source_target_pairs={{0,1},{1,2},{2,3},{3,4},{4,5},{5,6},{6,7},{7,0},{8,9},{9,10},{10,1... | collective-permute-start | bytes 442376 | tf_op jit(solution)/shard_map/ppermute | solution.py:361
  137.9 6.4 %collective-permute-start.29 = (bf16[144,512]{1,0:T(8,128)(2,1)S(1)}, bf16[144,512]{1,0:T(8,128)(2,1)S(1)}, u32[]{:S(2)}, u32[]{:S(2)}) collective-permute-start(bf16[144,512]{1,0:T(8,128)(2,1)S(1)} %add_convert_fusion.2), channel_id=1, source_target_pairs={{0,7},{1,0},{2,1},{3,2},{4,3},{5,4},{6,5},{7,6},{8,15},{9,8},{10,9... | collective-permute-start | bytes 442376 | tf_op jit(solution)/shard_map/ppermute | solution.py:361
  138.0 10.0 %collective-permute-start.22 = (bf16[144,512]{1,0:T(8,128)(2,1)S(1)}, bf16[144,512]{1,0:T(8,128)(2,1)S(1)}, u32[]{:S(2)}, u32[]{:S(2)}) collective-permute-start(bf16[144,512]{1,0:T(8,128)(2,1)S(1)} %add_convert_fusion.7), channel_id=1, source_target_pairs={{0,7},{1,0},{2,1},{3,2},{4,3},{5,4},{6,5},{7,6},{8,15},{9,8},{10,9... | collective-permute-start | bytes 442376 | tf_op jit(solution)/shard_map/ppermute | solution.py:361
  139.3 6.5 %copy-start.13 = (bf16[144,512]{1,0:T(8,128)(2,1)S(1)}, bf16[144,512]{1,0:T(8,128)(2,1)}, u32[]{:S(2)}) copy-start(bf16[144,512]{1,0:T(8,128)(2,1)} %copy-done.12) | copy-start | bytes 442372
  139.3 8.7 %copy-start.11 = (bf16[144,512]{1,0:T(8,128)(2,1)S(1)}, bf16[144,512]{1,0:T(8,128)(2,1)}, u32[]{:S(2)}) copy-start(bf16[144,512]{1,0:T(8,128)(2,1)} %copy-done.10) | copy-start | bytes 442372
  144.3 3.7 %collective-permute-start.34 = (f32[2,128]{1,0:T(2,128)S(1)}, f32[2,128]{1,0:T(2,128)S(1)}, u32[]{:S(2)}, u32[]{:S(2)}) collective-permute-start(f32[2,128]{1,0:T(2,128)S(1)} %convert_add_fusion.1), channel_id=1, source_target_pairs={{0,8},{1,9},{2,10},{3,11},{4,12},{5,13},{6,14},{7,15},{8,0},{9,1},... | collective-permute-start | bytes 3080 | tf_op jit(solution)/shard_map/ppermute | solution.py:365
  145.9 9.2 %collective-permute-start.33 = (bf16[128,512]{1,0:T(8,128)(2,1)S(1)}, bf16[128,512]{1,0:T(8,128)(2,1)S(1)}, u32[]{:S(2)}, u32[]{:S(2)}) collective-permute-start(bf16[128,512]{1,0:T(8,128)(2,1)S(1)} %add_convert_fusion.10), channel_id=1, source_target_pairs={{0,8},{1,9},{2,10},{3,11},{4,12},{5,13},{6,14},{7,15},{8,0},{9,1},... | collective-permute-start | bytes 393224 | tf_op jit(solution)/shard_map/ppermute | solution.py:365
  148.0 6.6 %collective-permute-start.35 = (f32[2,128]{1,0:T(2,128)S(1)}, f32[2,128]{1,0:T(2,128)S(1)}, u32[]{:S(2)}, u32[]{:S(2)}) collective-permute-start(f32[2,128]{1,0:T(2,128)S(1)} %add.124), channel_id=1, source_target_pairs={{0,240},{16,224},{32,208},{48,192},{64,176},{80,160},{96,144},{112... | collective-permute-start | bytes 3080 | tf_op jit(solution)/shard_map/ppermute | solution.py:438
  (11 other events, 7.2 us)
